TPU v7x, 32 devices: a whole 2x2x4 slice. The times are simulated.
32 devices in a mesh: dp: 16 (over z, y, x), seq: 2 (over core).
Axes of the slice: x: 2, y: 2, z: 4, core: 2. Of those that a mesh axis runs over, the one named last changes fastest.
Arguments:
- hidden_in: bfloat16 [4, 8192, 768], P(None, ('dp', 'seq')), may hold values from -6 to 6
- slot_sizes: int32 [16, 4, 8], P('dp'), may hold values from 0 to 512, as said below
- live_lengths: int32 [16, 4, 8], P('dp'), may hold values from 0 to 512, as said below
- w_query: bfloat16 [768, 768], replicated, may hold values from -0.21875 to 0.21875
- w_key: bfloat16 [768, 768], replicated, may hold values from -0.21875 to 0.21875
- w_value: bfloat16 [768, 768], replicated, may hold values from -0.21875 to 0.21875
- query_down_factor: bfloat16 [768, 8], replicated, may hold values from -0.21875 to 0.21875
- down_value: bfloat16 [768, 8], replicated, may hold values from -0.21875 to 0.21875
- query_up_factor: bfloat16 [8, 768], replicated, may hold values from -0.75 to 0.75
- value_up_factor: bfloat16 [8, 768], replicated, may hold values from -0.75 to 0.75
- w_output: bfloat16 [768, 768], replicated, may hold values from -1.75 to 1.75
- attn_gain: float32 [768], replicated, may hold values from 0.5 to 1.5
- attn_shift: float32 [768], replicated, may hold values from -4 to 4
- w_expand: bfloat16 [768, 3072], replicated, may hold values from -0.21875 to 0.21875
- w_reduce: bfloat16 [3072, 768], replicated, may hold values from -0.109375 to 0.109375
- ffn_gain: float32 [768], replicated, may hold values from 0.5 to 1.5
- ffn_shift: float32 [768], replicated, may hold values from -4 to 4
- out_grad: bfloat16 [4, 8192, 768], P(None, ('dp', 'seq')), may hold values from -6 to 6
Outputs:
- layer_out: bfloat16 [4, 8192, 768], P(None, ('dp', 'seq'))
- input_grad: float32 [4, 8192, 768], P(None, ('dp', 'seq'))
- up_query_grad: float32 [8, 768], replicated
- up_value_grad: float32 [8, 768], replicated
Inputs may be any that keep to these rules, and one draw needn't show every extreme that they name: `slot_sizes`: for each packed row the used slots come first, hold sizes 64, 128, 256 or 512 that sum to 512, the rest are 0; for each g one micro-batch holds a single item of 512 tokens. `live_lengths`: each entry lies between half of its slot's size (rounded up) and the size; 0 for unused slots; an item of 512 tokens is live throughout.
All inputs are finite; a program needn't handle non-finite values.
Results may differ from a plain program's by a relative error of at most 0.02.
Values may be sent and summed in bfloat16 or wider, within the bound.
A program may use at most 192 MiB of HBM per device.

v0:
```python
import functools
import math

import jax
import jax.numpy as jnp
from jax import lax
from jax.experimental import pallas as pl
from jax.experimental.pallas import tpu as pltpu
from jax.sharding import PartitionSpec as P

HEADS = 12
HEAD = 64
NORM_EPS = 1e-05
ADAPTER_STRENGTH = 16.0
MASK_FILL = -1e30
LOG2_E = math.log2(math.e)
LN_2 = math.log(2.0)
CHUNK = 512
BF16 = jnp.bfloat16
F32 = jnp.float32
MESH = pl.DeviceIdType.MESH
VMEM = pltpu.VMEM
HBM_SPEC = pl.BlockSpec(memory_space=pl.ANY)
VMEM_SPEC = pl.BlockSpec(memory_space=pltpu.VMEM)
SMEM_SPEC = pl.BlockSpec(memory_space=pltpu.SMEM)


def dot(left, right, over_left, over_right):
    return lax.dot_general(
        left, right, (((over_left,), (over_right,)), ((), ())), preferred_element_type=F32
    )


def project_kernel(
    hidden, out_grad, wq, wk, wv, aq, av, bq, bv,
    qt_out, k_out, kt_out, v_out, vt_out, low_out, x_out, og_out, wq_out, wv_out,
    x_own, x_got, wq_s, wk_s, wv_s, qt_s, k_s, kt_s, v_s, vt_s, load, store, send, recv, own_sem,
):
    micro, tokens, width = hidden.shape
    rows = micro // 2
    place = lax.axis_index("seq")
    other = 1 - place
    loads = [
        pltpu.make_async_copy(hidden.at[pl.ds(rows * place, rows)], x_own, load.at[0]),
        pltpu.make_async_copy(wq, wq_s, load.at[1]),
        pltpu.make_async_copy(wk, wk_s, load.at[2]),
        pltpu.make_async_copy(wv, wv_s, load.at[3]),
    ]
    for copy in loads:
        copy.start()
    barrier = pltpu.get_barrier_semaphore()
    pl.semaphore_signal(barrier, inc=1, device_id={"seq": other}, device_id_type=MESH)
    pl.semaphore_wait(barrier, 1)
    x_copy = pltpu.make_async_remote_copy(
        src_ref=hidden.at[pl.ds(rows * other, rows)], dst_ref=x_got,
        send_sem=send.at[0], recv_sem=recv.at[0],
        device_id={"seq": other}, device_id_type=MESH,
    )
    x_copy.start()
    og_copy = pltpu.make_async_remote_copy(
        src_ref=out_grad.at[pl.ds(rows * other, rows)], dst_ref=og_out,
        send_sem=send.at[1], recv_sem=recv.at[1],
        device_id={"seq": other}, device_id_type=MESH,
    )
    og_copy.start()
    strength = ADAPTER_STRENGTH / aq.shape[0]
    for copy in loads:
        copy.wait()
    wq_s[...] = (
        (wq_s[...].astype(F32) + strength * dot(aq[...], bq[...], 0, 0))
        * (LOG2_E / math.sqrt(HEAD))
    ).astype(BF16)
    wv_s[...] = (
        wv_s[...].astype(F32) + strength * dot(av[...], bv[...], 0, 0)
    ).astype(BF16)
    stores = []

    def keep(source, target):
        copy = pltpu.make_async_copy(source, target, store.at[len(stores)])
        copy.start()
        stores.append(copy)

    keep(wq_s, wq_out)
    keep(wv_s, wv_out)
    for half in range(2):
        if half == 1:
            x_copy.wait_recv()
            keep(x_got, x_out)
        x = (x_own if half == 0 else x_got)[...].reshape(rows * tokens, width)
        span = slice(half * tokens, (half + 1) * tokens)
        qt = dot(wq_s[...], x, 0, 1).astype(BF16)
        keys = dot(x, wk_s[...], 1, 0).astype(BF16)
        vt = dot(wv_s[...], x, 0, 1).astype(BF16)
        kt = keys.T
        values = vt.T
        low_q = dot(aq[...], x, 1, 1)
        low_v = dot(av[...], x, 1, 1)
        low = jnp.concatenate([low_q, low_v], axis=0).astype(BF16)
        for row in range(rows):
            part = slice(row * tokens, (row + 1) * tokens)
            qt_s[row, :, span] = qt[:, part]
            k_s[row, span, :] = keys[part, :]
            vt_s[row, :, span] = vt[:, part]
            kt_s[row, :, span] = kt[:, part]
            v_s[row, span, :] = values[part, :]
            low_out[row, :, span] = low[:, part]
        keep(qt_s.at[:, :, span], qt_out.at[:, :, span])
        keep(k_s.at[:, span], k_out.at[:, span])
        keep(vt_s.at[:, :, span], vt_out.at[:, :, span])
        keep(kt_s.at[:, :, span], kt_out.at[:, :, span])
        keep(v_s.at[:, span], v_out.at[:, span])
    for copy in stores:
        copy.wait()
    x_copy.wait_send()
    og_copy.wait()


def layer_kernel(
    sizes, lives, place_ref, gain_one, shift_one, gain_two, shift_two,
    hidden, out_grad, x_in, og_in, qt_in, k_in, kt_in, v_in, vt_in, low_in, wo_in, wx_in, wr_in,
    lo_out, g_out, dqt_out, dk_out, dv_out, up_out,
    x_s, og_s, qt_s, k_s, kt_s, v_s, vt_s, low_s, wo_s, wx_s, wr_s,
    probs, score, ctx_s, inv_s, gctx_s, normed_s, back_s, acc_s, low16, slope_s, act_s, ds_s, do_s,
    rstd_s, kmask, qmask, lo_s, g_s, dqt_s, dk_s, dv_s,
    load, weight_load, store,
):
    rows, group, width = x_s.shape
    tokens = group // 2
    hidden_units = wx_s.shape[1]
    place = place_ref[0]
    slots = sizes.shape[1]
    pairs = HEADS // 2
    gain_one, shift_one, gain_two, shift_two = (
        part[...].reshape(1, width) for part in (gain_one, shift_one, gain_two, shift_two)
    )

    def row_loads(row):
        own = rows * place + row
        first = pl.ds(0, tokens)
        second = pl.ds(tokens, tokens)
        plan = [
            (qt_in.at[row], qt_s.at[row]),
            (k_in.at[row], k_s.at[row]),
            (vt_in.at[row], vt_s.at[row]),
            (hidden.at[own], x_s.at[row, first]),
            (x_in.at[row], x_s.at[row, second]),
            (out_grad.at[own], og_s.at[row, first]),
            (og_in.at[row], og_s.at[row, second]),
            (v_in.at[row], v_s.at[row]),
            (kt_in.at[row], kt_s.at[row]),
            (low_in.at[row], low_s.at[row]),
        ]
        return [
            pltpu.make_async_copy(source, target, load.at[row, index])
            for index, (source, target) in enumerate(plan)
        ]

    weight_loads = [
        pltpu.make_async_copy(source, target, weight_load.at[index])
        for index, (source, target) in enumerate([(wo_in, wo_s), (wx_in, wx_s), (wr_in, wr_s)])
    ]
    first_loads = row_loads(0)
    for copy in first_loads[:3]:
        copy.start()
    weight_loads[0].start()
    for copy in first_loads[3:5]:
        copy.start()
    weight_loads[1].start()
    weight_loads[2].start()
    for copy in first_loads[5:]:
        copy.start()
    for row in range(1, rows):
        for copy in row_loads(row):
            copy.start()

    def row_stores(row):
        plan = [
            (lo_s.at[row], lo_out.at[row]),
            (g_s.at[row], g_out.at[row]),
            (dqt_s.at[row], dqt_out.at[row]),
            (dk_s.at[row], dk_out.at[row]),
            (dv_s.at[row], dv_out.at[row]),
        ]
        return [
            pltpu.make_async_copy(source, target, store.at[row, index])
            for index, (source, target) in enumerate(plan)
        ]

    def paired(top, bottom_zero):
        zero = jnp.zeros_like(top)
        return jnp.concatenate([top, zero] if bottom_zero else [zero, top], axis=0)

    def attend_forward(row, spans):
        def scores(head):
            pair, odd = divmod(head, 2)
            lanes = slice(pair * 128, pair * 128 + 128)
            query = qt_s[row, head * HEAD:(head + 1) * HEAD, :]
            right = jnp.concatenate([paired(query, odd == 0), qmask[...]], axis=0)
            for a, b in spans:
                left = jnp.concatenate([k_s[row, a:b, lanes], kmask[a:b, :]], axis=1)
                score[head % 2, a:b, a:b] = dot(left, right[:, a:b], 1, 0)

        def weights(head):
            for a, b in spans:
                part = score[head % 2, a:b, a:b]
                top = jnp.max(part, axis=0, keepdims=True)
                probs[head, a:b, a:b] = jnp.exp2(part - top).astype(BF16)

        def contexts(head):
            values = vt_s[row, head * HEAD:(head + 1) * HEAD, :]
            left = jnp.concatenate([values, jnp.ones((16, group), BF16)], axis=0)
            for a, b in spans:
                total = dot(left[:, a:b], probs[head, a:b, a:b], 1, 0)
                inverse = 1.0 / total[HEAD:HEAD + 1]
                inv_s[head:head + 1, a:b] = inverse
                ctx_s[head * HEAD:(head + 1) * HEAD, a:b] = (total[:HEAD] * inverse).astype(BF16)

        for step in range(HEADS + 2):
            if step < HEADS:
                scores(step)
            if 0 <= step - 1 < HEADS:
                weights(step - 1)
            if 0 <= step - 2:
                contexts(step - 2)

    def attend_backward(row, spans):
        def score_grads(head):
            pair, odd = divmod(head, 2)
            lanes = slice(pair * 128, pair * 128 + 128)
            here = slice(head * HEAD, (head + 1) * HEAD)
            slot = head % 4
            grad = gctx_s[here, :] * inv_s[head:head + 1, :]
            short = grad.astype(BF16)
            do_s[slot] = short
            delta = -jnp.sum(grad * ctx_s[here, :].astype(F32), axis=0, keepdims=True)
            high = delta.astype(BF16).astype(F32)
            index = lax.broadcasted_iota(jnp.int32, (16, group), 0)
            extra = jnp.where(index == 0, high, jnp.where(index == 1, delta - high, 0.0))
            right = jnp.concatenate(
                [paired(short, odd == 0), extra.astype(BF16), jnp.zeros((112, group), BF16)], axis=0
            )
            for a, b in spans:
                left = jnp.concatenate(
                    [v_s[row, a:b, lanes], jnp.ones((b - a, 128), BF16)], axis=1
                )
                part = dot(left, right[:, a:b], 1, 0)
                ds_s[slot, a:b, a:b] = (probs[head, a:b, a:b].astype(F32) * part).astype(BF16)

        def grads(pair):
            lanes = slice(pair * 128, pair * 128 + 128)
            even, odd = 2 * pair, 2 * pair + 1
            for a, b in spans:
                for head in (even, odd):
                    here = slice(head * HEAD, (head + 1) * HEAD)
                    dqt_s[row, here, a:b] = (
                        dot(kt_s[row, here, a:b], ds_s[head % 4, a:b, a:b], 1, 0) * LN_2
                    ).astype(BF16)
                left = jnp.concatenate([ds_s[even % 4, a:b, a:b], ds_s[odd % 4, a:b, a:b]], axis=1)
                right = jnp.concatenate(
                    [
                        paired(qt_s[row, even * HEAD:even * HEAD + HEAD, a:b], True),
                        paired(qt_s[row, odd * HEAD:odd * HEAD + HEAD, a:b], False),
                    ],
                    axis=1,
                )
                dk_s[row, a:b, lanes] = (dot(left, right, 1, 1) * LN_2).astype(BF16)
                left = jnp.concatenate([probs[even, a:b, a:b], probs[odd, a:b, a:b]], axis=1)
                right = jnp.concatenate(
                    [paired(do_s[even % 4, :, a:b], True), paired(do_s[odd % 4, :, a:b], False)],
                    axis=1,
                )
                dv_s[row, a:b, lanes] = dot(left, right, 1, 1).astype(BF16)

        for step in range(pairs + 1):
            if step < pairs:
                score_grads(2 * step)
                score_grads(2 * step + 1)
            if step >= 1:
                grads(step - 1)

    def mean(value):
        return jnp.sum(value, axis=-1, keepdims=True) * (1.0 / width)

    def by_blocks(body, block=64):
        def step(index, carry):
            body(pl.ds(pl.multiple_of(index * block, block), block))
            return carry

        lax.fori_loop(0, group // block, step, 0)

    def one_row(row, carry):
        own = rows * place + row
        position = (lax.broadcasted_iota(jnp.int32, (group, 128), 0) + place * tokens) % group
        lane = lax.broadcasted_iota(jnp.int32, (1, 128), 1)
        low = jnp.full((1, 128), group, jnp.int32)
        high = low
        across = lax.broadcasted_iota(jnp.int32, (slots, group), 1)
        across = (across + place * tokens) % group
        line = lax.broadcasted_iota(jnp.int32, (slots, 1), 0)
        first = jnp.full((slots, 1), group, jnp.int32)
        last = first
        start = jnp.int32(0)
        crossing = jnp.int32(0)
        for slot in range(slots):
            size = sizes[own, slot]
            live = lives[own, slot]
            low = jnp.where(lane == slot, start, low)
            high = jnp.where(lane == slot, start + live, high)
            first = jnp.where(line == slot, start, first)
            last = jnp.where(line == slot, start + size, last)
            over = (start < tokens) & (start + size > tokens)
            crossing = jnp.where(over, 1, crossing)
            start = start + size
        dead = jnp.where((position >= low) & (position < high), 0.0, 1.0)
        kmask[...] = jnp.where(lane < slots, dead, 0.0).astype(BF16)
        within = jnp.where((across >= first) & (across < last), MASK_FILL, 0.0)
        qmask[...] = jnp.concatenate(
            [within, jnp.zeros((128 - slots, group), F32)], axis=0
        ).astype(BF16)

        loads = row_loads(row)
        for copy in loads[:3]:
            copy.wait()

        @pl.when(crossing == 1)
        def _():
            attend_forward(row, [(0, group)])

        @pl.when(crossing == 0)
        def _():
            attend_forward(row, [(0, tokens), (tokens, group)])

        @pl.when(row == 0)
        def _():
            weight_loads[0].wait()

        for copy in loads[3:5]:
            copy.wait()
        acc_s[...] = dot(ctx_s[...], wo_s[...], 0, 0)

        def norm_one(at):
            resid = x_s[row, at, :].astype(F32) + acc_s[at, :]
            center = resid - mean(resid)
            scaled = lax.rsqrt(mean(center * center) + NORM_EPS)
            normed = center * scaled
            normed_s[at, :] = normed
            rstd_s[at, :] = scaled
            low16[at, :] = (normed * gain_one + shift_one).astype(BF16)

        by_blocks(norm_one)

        @pl.when(row == 0)
        def _():
            weight_loads[1].wait()
            weight_loads[2].wait()

        chunks = hidden_units // CHUNK
        for step in range(chunks + 2):
            if step < chunks:
                at = slice(step * CHUNK, (step + 1) * CHUNK)
                score[step % 2] = dot(low16[...], wx_s[:, at], 1, 0)
            if 0 <= step - 1 < chunks:
                at = slice((step - 1) * CHUNK, step * CHUNK)
                inner = score[(step - 1) % 2]
                upto = 0.5 + 0.5 * lax.erf(inner * math.sqrt(0.5))
                bell = jnp.exp2(inner * inner * (-0.5 * LOG2_E)) * (1.0 / math.sqrt(2.0 * math.pi))
                act_s[(step - 1) % 2] = (inner * upto).astype(BF16)
                slope_s[:, at] = (upto + inner * bell).astype(BF16)
            if 0 <= step - 2:
                at = slice((step - 2) * CHUNK, (step - 1) * CHUNK)
                part = dot(act_s[(step - 2) % 2], wr_s[at, :], 1, 0)
                if step == 2:
                    acc_s[...] = part
                else:
                    acc_s[...] += part

        for copy in loads[5:7]:
            copy.wait()

        def norm_two(at):
            z = normed_s[at, :] * gain_one + shift_one + acc_s[at, :]
            center = z - mean(z)
            scaled = lax.rsqrt(mean(center * center) + NORM_EPS)
            normed = center * scaled
            lo_s[row, at, :] = (normed * gain_two + shift_two).astype(BF16)
            weighted = og_s[row, at, :].astype(F32) * gain_two
            grad = scaled * (weighted - mean(weighted) - normed * mean(weighted * normed))
            back_s[at, :] = grad
            low16[at, :] = grad.astype(BF16)

        by_blocks(norm_two)
        for step in range(chunks + 1):
            if step < chunks:
                at = slice(step * CHUNK, (step + 1) * CHUNK)
                part = dot(low16[...], wr_s[at, :], 1, 1)
                act_s[step % 2] = (part * slope_s[:, at].astype(F32)).astype(BF16)
            if step >= 1:
                at = slice((step - 1) * CHUNK, step * CHUNK)
                part = dot(act_s[(step - 1) % 2], wx_s[:, at], 1, 1)
                if step == 1:
                    acc_s[...] = part
                else:
                    acc_s[...] += part

        def norm_one_back(at):
            weighted = (back_s[at, :] + acc_s[at, :]) * gain_one
            normed = normed_s[at, :]
            grad = rstd_s[at, :] * (
                weighted - mean(weighted) - normed * mean(weighted * normed)
            )
            g_s[row, at, :] = grad.astype(BF16)

        by_blocks(norm_one_back)
        gctx_s[...] = dot(wo_s[...], g_s[row], 1, 1)
        for copy in loads[7:]:
            copy.wait()

        @pl.when(crossing == 1)
        def _():
            attend_backward(row, [(0, group)])

        @pl.when(crossing == 0)
        def _():
            attend_backward(row, [(0, tokens), (tokens, group)])

        for copy in row_stores(row):
            copy.start()
        from_q = dot(low_s[row], dqt_s[row], 1, 1) * (
            ADAPTER_STRENGTH / slots_rank / math.sqrt(HEAD) / LN_2
        )
        from_v = dot(low_s[row], dv_s[row], 1, 0) * (ADAPTER_STRENGTH / slots_rank)
        rank_line = lax.broadcasted_iota(jnp.int32, (2 * slots_rank, 1), 0)
        part = jnp.where(rank_line < slots_rank, from_q, from_v)
        up_out[...] = jnp.where(row == 0, part, up_out[...] + part)
        return carry

    slots_rank = low_s.shape[1] // 2
    lax.fori_loop(0, rows, one_row, 0)
    for row in range(rows):
        for copy in row_stores(row):
            copy.wait()


def partners():
    found = [("seq", 1)]
    bit = 1
    while bit < lax.axis_size("dp"):
        found.append(("dp", bit))
        bit *= 2
    return found


def finish_kernel(
    up, lo, grad, dqt, dk, dv, wq, wk, wv,
    lo_out, ig_out, upq_out, upv_out,
    total, got, grad_s, dqt_s, dk_s, dv_s, wq_s, wk_s, wv_s, res_s,
    load, store, send, recv, ar_send, ar_recv,
):
    rows, group, width = grad.shape
    tokens = group // 2
    place = lax.axis_index("seq")
    other = 1 - place
    plan = [
        (wq, wq_s), (wk, wk_s), (wv, wv_s),
        (dqt, dqt_s), (dk, dk_s), (dv, dv_s), (grad, grad_s),
    ]
    loads = [
        pltpu.make_async_copy(source, target, load.at[index])
        for index, (source, target) in enumerate(plan)
    ]
    for copy in loads:
        copy.start()
    barrier = pltpu.get_barrier_semaphore()
    rounds = []
    for axis, bit in partners():
        me = lax.axis_index(axis)
        rounds.append({axis: me + bit - 2 * bit * ((me // bit) % 2)})
    for partner in rounds:
        pl.semaphore_signal(barrier, inc=1, device_id=partner, device_id_type=MESH)
    pl.semaphore_wait(barrier, len(rounds))
    mine = pl.ds(rows * place, rows)
    lo_copy = pltpu.make_async_remote_copy(
        src_ref=lo.at[:, pl.ds(tokens, tokens)], dst_ref=lo_out.at[mine],
        send_sem=send.at[0], recv_sem=recv.at[0],
        device_id={"seq": other}, device_id_type=MESH,
    )
    reduces = [
        pltpu.make_async_remote_copy(
            src_ref=total.at[index], dst_ref=got.at[index],
            send_sem=ar_send.at[index], recv_sem=ar_recv.at[index],
            device_id=partner, device_id_type=MESH,
        )
        for index, partner in enumerate(rounds)
    ]
    total[0] = up[...]
    reduces[0].start()
    lo_copy.start()
    keep_lo = pltpu.make_async_copy(lo.at[:, pl.ds(0, tokens)], lo_out.at[mine], store.at[0])
    keep_lo.start()
    done = [0]

    def advance():
        index = done[0]
        if index == len(rounds):
            return
        reduces[index].wait_recv()
        total[index + 1] = total[index] + got[index]
        done[0] = index + 1
        if index + 1 < len(rounds):
            reduces[index + 1].start()

    for copy in loads:
        copy.wait()

    def piece(half, block):
        span = slice(half * tokens, (half + 1) * tokens)
        outs = slice(block * 256, block * 256 + 256)
        left_q = jnp.concatenate([dqt_s[row, :, span] for row in range(rows)], axis=1)
        left_k = dk_s[:, span, :].reshape(rows * tokens, width)
        left_v = dv_s[:, span, :].reshape(rows * tokens, width)
        value = dot(left_q, wq_s[outs, :], 0, 1)
        value += dot(left_k, wk_s[outs, :], 1, 1)
        value += dot(left_v, wv_s[outs, :], 1, 1)
        value += grad_s[:, span, outs].reshape(rows * tokens, 256).astype(F32)
        res_s[half, :, :, outs] = value.astype(BF16).reshape(rows, tokens, 256)

    blocks = width // 256
    for block in range(blocks):
        piece(1, block)
        advance()
    ig_copy = pltpu.make_async_remote_copy(
        src_ref=res_s.at[1], dst_ref=ig_out.at[mine],
        send_sem=send.at[1], recv_sem=recv.at[1],
        device_id={"seq": other}, device_id_type=MESH,
    )
    ig_copy.start()
    for block in range(blocks):
        piece(0, block)
        advance()
    keep_ig = pltpu.make_async_copy(res_s.at[0], ig_out.at[mine], store.at[1])
    keep_ig.start()
    for _ in range(len(rounds)):
        advance()
    last = total[len(rounds)]
    rank = up.shape[0] // 2
    upq_out[...] = last[:rank]
    upv_out[...] = last[rank:]
    for copy in reduces:
        copy.wait_send()
    keep_lo.wait()
    keep_ig.wait()
    lo_copy.wait()
    ig_copy.wait()


def shards(
    hidden_in, slot_sizes, live_lengths, w_query, w_key, w_value, query_down_factor, down_value,
    query_up_factor, value_up_factor, w_output, attn_gain, attn_shift, w_expand, w_reduce,
    ffn_gain, ffn_shift, out_grad,
):
    micro, tokens, width = hidden_in.shape
    rows = micro // 2
    group = 2 * tokens
    hidden_units = w_expand.shape[1]
    rank = query_down_factor.shape[1]
    shape = jax.ShapeDtypeStruct
    dma = pltpu.SemaphoreType.DMA
    wide = (rows, width, group)
    tall = (rows, group, width)
    mega = 2 ** 20
    qt, keys, kt, values, vt, low, x_got, og_got, wq_eff, wv_eff = pl.pallas_call(
        project_kernel,
        out_shape=[
            shape(wide, BF16), shape(tall, BF16), shape(wide, BF16), shape(tall, BF16),
            shape(wide, BF16), shape((rows, 2 * rank, group), BF16),
            shape((rows, tokens, width), BF16), shape((rows, tokens, width), BF16),
            shape((width, width), BF16), shape((width, width), BF16),
        ],
        in_specs=[HBM_SPEC] * 5 + [VMEM_SPEC] * 4,
        out_specs=[HBM_SPEC] * 5 + [VMEM_SPEC] + [HBM_SPEC] * 4,
        scratch_shapes=[
            VMEM((rows, tokens, width), BF16), VMEM((rows, tokens, width), BF16),
            VMEM((width, width), BF16), VMEM((width, width), BF16), VMEM((width, width), BF16),
            VMEM(wide, BF16), VMEM(tall, BF16), VMEM(wide, BF16), VMEM(tall, BF16),
            VMEM(wide, BF16),
            dma((4,)), dma((13,)), dma((2,)), dma((2,)), dma((1,)),
        ],
        compiler_params=pltpu.CompilerParams(
            collective_id=0, has_side_effects=True, vmem_limit_bytes=62 * mega
        ),
        name="project",
    )(
        hidden_in, out_grad, w_query, w_key, w_value, query_down_factor.T, down_value.T,
        query_up_factor, value_up_factor,
    )
    place = lax.axis_index("seq").astype(jnp.int32).reshape(1)
    lo, grad, dqt, dk, dv, up = pl.pallas_call(
        layer_kernel,
        out_shape=[
            shape(tall, BF16), shape(tall, BF16), shape(wide, BF16), shape(tall, BF16),
            shape(tall, BF16), shape((2 * rank, width), F32),
        ],
        in_specs=[SMEM_SPEC] * 3 + [VMEM_SPEC] * 4 + [HBM_SPEC] * 13,
        out_specs=[HBM_SPEC] * 5 + [VMEM_SPEC],
        scratch_shapes=[
            VMEM(tall, BF16), VMEM(tall, BF16), VMEM(wide, BF16), VMEM(tall, BF16),
            VMEM(wide, BF16), VMEM(tall, BF16), VMEM(wide, BF16),
            VMEM((rows, 2 * rank, group), BF16),
            VMEM((width, width), BF16), VMEM((width, hidden_units), BF16),
            VMEM((hidden_units, width), BF16),
            VMEM((HEADS, group, group), BF16), VMEM((2, group, group), F32),
            VMEM((width, group), BF16), VMEM((16, group), F32), VMEM((width, group), F32),
            VMEM((group, width), F32), VMEM((group, width), F32), VMEM((group, width), F32),
            VMEM((group, width), BF16), VMEM((group, hidden_units), BF16),
            VMEM((2, group, CHUNK), BF16), VMEM((4, group, group), BF16),
            VMEM((4, HEAD, group), BF16), VMEM((group, 1), F32),
            VMEM((group, 128), BF16), VMEM((128, group), BF16),
            VMEM(tall, BF16), VMEM(tall, BF16), VMEM(wide, BF16), VMEM(tall, BF16),
            VMEM(tall, BF16),
            dma((rows, 10)), dma((3,)), dma((rows, 5)),
        ],
        compiler_params=pltpu.CompilerParams(vmem_limit_bytes=62 * mega),
        name="layer",
    )(
        slot_sizes[0], live_lengths[0], place, attn_gain, attn_shift, ffn_gain, ffn_shift, hidden_in, out_grad, x_got, og_got,
        qt, keys, kt, values, vt, low, w_output, w_expand, w_reduce,
    )
    count = len(partners())
    layer_out, input_grad, up_query_grad, up_value_grad = pl.pallas_call(
        finish_kernel,
        out_shape=[
            shape((micro, tokens, width), BF16), shape((micro, tokens, width), BF16),
            shape((rank, width), F32), shape((rank, width), F32),
        ],
        in_specs=[VMEM_SPEC] + [HBM_SPEC] * 8,
        out_specs=[HBM_SPEC] * 2 + [VMEM_SPEC] * 2,
        scratch_shapes=[
            VMEM((count + 1, 2 * rank, width), F32), VMEM((count, 2 * rank, width), F32),
            VMEM(tall, BF16), VMEM(wide, BF16), VMEM(tall, BF16), VMEM(tall, BF16),
            VMEM((width, width), BF16), VMEM((width, width), BF16), VMEM((width, width), BF16),
            VMEM((2, rows, tokens, width), BF16),
            dma((7,)), dma((2,)), dma((2,)), dma((2,)), dma((count,)), dma((count,)),
        ],
        compiler_params=pltpu.CompilerParams(
            collective_id=1, has_side_effects=True, vmem_limit_bytes=62 * mega
        ),
        name="finish",
    )(up, lo, grad, dqt, dk, dv, wq_eff, w_key, wv_eff)
    return layer_out, input_grad.astype(F32), up_query_grad, up_value_grad


def solution(mesh):
    tokens = P(None, ("dp", "seq"), None)
    table = P("dp", None, None)
    in_specs = (tokens, table, table) + (P(),) * 14 + (tokens,)
    out_specs = (tokens, tokens, P(), P())
    return jax.shard_map(shards, mesh=mesh, in_specs=in_specs, out_specs=out_specs, check_vma=False)
```

profile of v0, /device:TPU:0, one launch (start us, length us, event | category | flops | bytes accessed | tf_op | source)
XLA Modules:
  0.0 105.2 jit_solution(10475497709230052251)
XLA Ops:
  0.6 10.5 %project.1 = (bf16[2,768,512]{2,1,0:T(8,128)(2,1)}, bf16[2,512,768]{2,1,0:T(8,128)(2,1)}, bf16[2,768,512]{2,1,0:T(8,128)(2,1)}, bf16[2,512,768]{2,1,0:T(8,128)(2...) custom-call(bf16[4,256,768]{2,1,0:T(8,128)(2,1)} %hidden.3, ...), custom_call_target="tpu_custom_call" | custom-call | tf_op jit(solution)/shard_map/project/pallas_call | solution.py:571
  11.1 57.5 %layer.1 = (bf16[2,512,768]{2,1,0:T(8,128)(2,1)}, bf16[2,512,768]{2,1,0:T(8,128)(2,1)}, bf16[2,768,512]{2,1,0:T(8,128)(2,1)}, bf16[2,512,768]{2,1,0:T(8,128)(2,1...) custom-call(s32[4,8]{1,0:T(4,128)} %bitcast.7, s32[4,8]{1,0:T(4,128)} %bitcast.8, s32[1]{0:T(128)} %bitcast.2.place_ref, ...), custom_call_target="tpu_custom_call" | custom-call | tf_op jit(solution)/shard_map/layer/pallas_call | solution.py:597
  68.6 30.7 %finish.1 = (bf16[4,256,768]{2,1,0:T(8,128)(2,1)}, bf16[4,256,768]{2,1,0:T(8,128)(2,1)}, f32[8,768]{1,0:T(8,128)}, f32[8,768]{1,0:T(8,128)}) custom-call(f32[16,768]{1,0:T(8,128)} %get-tuple-element.32.up, bf16[2,512,768]{2,1,0:T(8,128)(2,1)} %get-tuple-element.33.lo, bf16[2,512,768]{2,1,0:T(8,128)(2,1)} %get-tuple-element.34.grad, ...), custom_call_target="tpu_custom_call" | custom-call | tf_op jit(solution)/shard_map/finish/pallas_call | solution.py:629
  99.3 0.0 copy-start
  99.3 3.5 %convert_element_type.3 = f32[4,256,768]{2,1,0:T(8,128)} convert(bf16[4,256,768]{2,1,0:T(8,128)(2,1)} %get-tuple-element.41) | non-fusion elementwise | flops 786432 | bytes 4718592 | tf_op jit(solution)/shard_map/convert_element_type | solution.py:649
  102.8 0.0 copy-done
  102.8 0.0 copy-start.2
  102.8 0.0 copy-start.1
  102.8 1.1 %copy.25 = bf16[4,256,768]{2,1,0:T(8,128)(2,1)} copy(bf16[4,256,768]{2,1,0:T(8,128)(2,1)S(1)} %copy-done) | data formatting | bytes 3145728
  103.9 0.0 copy-done.2
  103.9 0.6 copy.26
  104.5 0.0 copy-done.1
  104.5 0.6 copy.27
Async XLA Ops:
  99.3 3.5 %copy-start = (bf16[4,256,768]{2,1,0:T(8,128)(2,1)S(1)}, bf16[4,256,768]{2,1,0:T(8,128)(2,1)}, u32[]{:S(2)}) copy-start(bf16[4,256,768]{2,1,0:T(8,128)(2,1)} %get-tuple-element.48) | copy-start | bytes 4718596
  102.8 1.1 %copy-start.2 = (f32[8,768]{1,0:T(8,128)S(1)}, f32[8,768]{1,0:T(8,128)}, u32[]{:S(2)}) copy-start(f32[8,768]{1,0:T(8,128)} %get-tuple-element.50) | copy-start | bytes 73732
  102.8 1.8 %copy-start.1 = (f32[8,768]{1,0:T(8,128)S(1)}, f32[8,768]{1,0:T(8,128)}, u32[]{:S(2)}) copy-start(f32[8,768]{1,0:T(8,128)} %get-tuple-element.51) | copy-start | bytes 73732
where the time goes:
time: 106 us; the launch traced here: 105 us
  Pallas kernels  98.7 us (93%)
  other arithmetic  3.45 us (3%)
  local copies, waits for them, and re-layouts  2.37 us (2%)
    pallas_call x1, Pallas kernels, shards(): pl.pallas_call(layer_kernel, out_shape=[shape(tall, BF16), shape(tall, BF...  57.5 us
    pallas_call x1, Pallas kernels, shards(): pl.pallas_call(finish_kernel, out_shape=[shape((micro, tokens, width), BF...  30.7 us
    pallas_call x1, Pallas kernels, shards(): pl.pallas_call(project_kernel, out_shape=[shape(wide, BF16), shape(tall,...  10.5 us
    convert_element_type x1, other arithmetic, shards(): return (layer_out, input_grad.astype(F32), up_query_grad, up_value_grad)  3.45 us
    unnamed x9, local copies, waits for them, and re-layouts  2.37 us

commit v1 on v0

v1 whole, which is shorter than its diff:
```python
import functools
import math

import jax
import jax.numpy as jnp
from jax import lax
from jax.experimental import pallas as pl
from jax.experimental.pallas import tpu as pltpu
from jax.sharding import PartitionSpec as P

HEADS = 12
HEAD = 64
NORM_EPS = 1e-05
ADAPTER_STRENGTH = 16.0
MASK_FILL = -1e30
LOG2_E = math.log2(math.e)
LN_2 = math.log(2.0)
CHUNK = 512
BF16 = jnp.bfloat16
F32 = jnp.float32
MESH = pl.DeviceIdType.MESH
VMEM = pltpu.VMEM
HBM_SPEC = pl.BlockSpec(memory_space=pl.ANY)
VMEM_SPEC = pl.BlockSpec(memory_space=pltpu.VMEM)
SMEM_SPEC = pl.BlockSpec(memory_space=pltpu.SMEM)


def dot(left, right, over_left, over_right):
    return lax.dot_general(
        left, right, (((over_left,), (over_right,)), ((), ())), preferred_element_type=F32
    )


def exchange_kernel(
    hidden, out_grad, wq, wk, wv, aq, av, bq, bv,
    x_out, og_out, qt_out, k_out, vt_out, low_out, wq_out, wv_out,
    x_s, wq_s, wk_s, wv_s, qt_s, k_s, vt_s, load, store, send, recv,
):
    rows, tokens, width = x_s.shape
    place = lax.axis_index("seq")
    other = 1 - place
    loads = [
        pltpu.make_async_copy(source, target, load.at[index])
        for index, (source, target) in enumerate([
            (wq, wq_s), (hidden.at[pl.ds(rows * place, rows)], x_s), (wk, wk_s), (wv, wv_s),
        ])
    ]
    for copy in loads:
        copy.start()
    barrier = pltpu.get_barrier_semaphore()
    pl.semaphore_signal(barrier, inc=1, device_id={"seq": other}, device_id_type=MESH)
    pl.semaphore_wait(barrier, 1)
    remote = [
        pltpu.make_async_remote_copy(
            src_ref=source.at[pl.ds(rows * other, rows)], dst_ref=target,
            send_sem=send.at[index], recv_sem=recv.at[index],
            device_id={"seq": other}, device_id_type=MESH,
        )
        for index, (source, target) in enumerate([(hidden, x_out), (out_grad, og_out)])
    ]
    for copy in remote:
        copy.start()
    strength = ADAPTER_STRENGTH / aq.shape[0]
    stores = []

    def keep(source, target):
        copy = pltpu.make_async_copy(source, target, store.at[len(stores)])
        copy.start()
        stores.append(copy)

    loads[0].wait()
    wq_s[...] = (
        (wq_s[...].astype(F32) + strength * dot(aq[...], bq[...], 0, 0))
        * (LOG2_E / math.sqrt(HEAD))
    ).astype(BF16)
    keep(wq_s, wq_out)
    loads[1].wait()
    x = x_s[...].reshape(rows * tokens, width)
    qt = dot(wq_s[...], x, 0, 1).astype(BF16)
    for row in range(rows):
        qt_s[row] = qt[:, row * tokens:(row + 1) * tokens]
    keep(qt_s, qt_out)
    loads[3].wait()
    wv_s[...] = (
        wv_s[...].astype(F32) + strength * dot(av[...], bv[...], 0, 0)
    ).astype(BF16)
    keep(wv_s, wv_out)
    loads[2].wait()
    k_s[...] = dot(x, wk_s[...], 1, 0).astype(BF16).reshape(rows, tokens, width)
    keep(k_s, k_out)
    vt = dot(wv_s[...], x, 0, 1).astype(BF16)
    for row in range(rows):
        vt_s[row] = vt[:, row * tokens:(row + 1) * tokens]
    keep(vt_s, vt_out)
    low = jnp.concatenate([dot(aq[...], x, 1, 1), dot(av[...], x, 1, 1)], axis=0).astype(BF16)
    for row in range(rows):
        low_out[row] = low[:, row * tokens:(row + 1) * tokens]
    for copy in stores:
        copy.wait()
    for copy in remote:
        copy.wait()


def layer_kernel(
    sizes, lives, place_ref, gain_one, shift_one, gain_two, shift_two, low_in, aq, av,
    hidden, out_grad, x_in, og_in, qt_in, k_in, vt_in, wq_in, wk_in, wv_in, wo_in, wx_in, wr_in,
    lo_out, g_out, dqt_out, dk_out, dv_out, up_out,
    x_s, og_s, qt_s, k_s, vt_s, kt_s, v_s, low_s, wq_s, wk_s, wv_s, wo_s, wx_s, wr_s,
    probs, score, ctx_s, inv_s, gctx_s, normed_s, back_s, acc_s, low16, slope_s, act_s, ds_s, do_s,
    rstd_s, kmask, qmask, lo_s, g_s, dqt_s, dk_s, dv_s,
    load, store,
):
    rows, group, width = x_s.shape
    tokens = group // 2
    hidden_units = wx_s.shape[1]
    place = place_ref[0]
    slots = sizes.shape[1]
    pairs = HEADS // 2
    gain_one, shift_one, gain_two, shift_two = (
        part[...].reshape(1, width) for part in (gain_one, shift_one, gain_two, shift_two)
    )
    first = pl.ds(0, tokens)
    second = pl.ds(tokens, tokens)
    mine = pl.ds(rows * place, rows)
    loads = [
        pltpu.make_async_copy(source, target, load.at[index])
        for index, (source, target) in enumerate([
            (x_in, x_s.at[:, second]),
            (wk_in, wk_s),
            (wq_in, wq_s),
            (wv_in, wv_s),
            (qt_in, qt_s.at[:, :, first]),
            (k_in, k_s.at[:, first]),
            (vt_in, vt_s.at[:, :, first]),
            (wo_in, wo_s),
            (hidden.at[mine], x_s.at[:, first]),
            (wx_in, wx_s),
            (wr_in, wr_s),
            (out_grad.at[mine], og_s.at[:, first]),
            (og_in, og_s.at[:, second]),
        ])
    ]
    for copy in loads:
        copy.start()

    def row_stores(row):
        plan = [
            (lo_s.at[row], lo_out.at[row]),
            (g_s.at[row], g_out.at[row]),
            (dqt_s.at[row], dqt_out.at[row]),
            (dk_s.at[row], dk_out.at[row]),
            (dv_s.at[row], dv_out.at[row]),
        ]
        return [
            pltpu.make_async_copy(source, target, store.at[row, index])
            for index, (source, target) in enumerate(plan)
        ]

    loads[0].wait()
    loads[1].wait()
    x = x_s[:, tokens:, :].reshape(rows * tokens, width)
    k_s[:, tokens:, :] = dot(x, wk_s[...], 1, 0).astype(BF16).reshape(rows, tokens, width)
    low = jnp.concatenate([dot(aq[...], x, 1, 1), dot(av[...], x, 1, 1)], axis=0).astype(BF16)
    for row in range(rows):
        low_s[row, :, :tokens] = low_in[row]
        low_s[row, :, tokens:] = low[:, row * tokens:(row + 1) * tokens]
    for weight, target, copy in ((wq_s, qt_s, loads[2]), (wv_s, vt_s, loads[3])):
        copy.wait()
        part = dot(weight[...], x, 0, 1).astype(BF16)
        for row in range(rows):
            target[row, :, tokens:] = part[:, row * tokens:(row + 1) * tokens]
    for copy in loads[4:7]:
        copy.wait()

    def paired(top, bottom_zero):
        zero = jnp.zeros_like(top)
        return jnp.concatenate([top, zero] if bottom_zero else [zero, top], axis=0)

    def attend_forward(row, spans):
        def scores(head):
            pair, odd = divmod(head, 2)
            lanes = slice(pair * 128, pair * 128 + 128)
            query = qt_s[row, head * HEAD:(head + 1) * HEAD, :]
            right = jnp.concatenate([paired(query, odd == 0), qmask[...]], axis=0)
            for a, b in spans:
                left = jnp.concatenate([k_s[row, a:b, lanes], kmask[a:b, :]], axis=1)
                score[head % 2, a:b, a:b] = dot(left, right[:, a:b], 1, 0)

        def weights(head):
            for a, b in spans:
                part = score[head % 2, a:b, a:b]
                top = jnp.max(part, axis=0, keepdims=True)
                probs[head, a:b, a:b] = jnp.exp2(part - top).astype(BF16)

        def contexts(head):
            values = vt_s[row, head * HEAD:(head + 1) * HEAD, :]
            left = jnp.concatenate([values, jnp.ones((16, group), BF16)], axis=0)
            for a, b in spans:
                total = dot(left[:, a:b], probs[head, a:b, a:b], 1, 0)
                inverse = 1.0 / total[HEAD:HEAD + 1]
                inv_s[head:head + 1, a:b] = inverse
                ctx_s[head * HEAD:(head + 1) * HEAD, a:b] = (total[:HEAD] * inverse).astype(BF16)

        for step in range(HEADS + 2):
            if step < HEADS:
                scores(step)
            if 0 <= step - 1 < HEADS:
                weights(step - 1)
            if 0 <= step - 2:
                contexts(step - 2)

    def attend_backward(row, spans):
        def score_grads(head):
            pair, odd = divmod(head, 2)
            lanes = slice(pair * 128, pair * 128 + 128)
            here = slice(head * HEAD, (head + 1) * HEAD)
            slot = head % 4
            grad = gctx_s[here, :] * inv_s[head:head + 1, :]
            short = grad.astype(BF16)
            do_s[slot] = short
            delta = -jnp.sum(grad * ctx_s[here, :].astype(F32), axis=0, keepdims=True)
            high = delta.astype(BF16).astype(F32)
            index = lax.broadcasted_iota(jnp.int32, (16, group), 0)
            extra = jnp.where(index == 0, high, jnp.where(index == 1, delta - high, 0.0))
            right = jnp.concatenate(
                [paired(short, odd == 0), extra.astype(BF16), jnp.zeros((112, group), BF16)], axis=0
            )
            for a, b in spans:
                left = jnp.concatenate(
                    [v_s[a:b, lanes], jnp.ones((b - a, 128), BF16)], axis=1
                )
                part = dot(left, right[:, a:b], 1, 0)
                ds_s[slot, a:b, a:b] = (probs[head, a:b, a:b].astype(F32) * part).astype(BF16)

        def grads(pair):
            lanes = slice(pair * 128, pair * 128 + 128)
            even, odd = 2 * pair, 2 * pair + 1
            for a, b in spans:
                for head in (even, odd):
                    here = slice(head * HEAD, (head + 1) * HEAD)
                    dqt_s[row, here, a:b] = (
                        dot(kt_s[here, a:b], ds_s[head % 4, a:b, a:b], 1, 0) * LN_2
                    ).astype(BF16)
                left = jnp.concatenate([ds_s[even % 4, a:b, a:b], ds_s[odd % 4, a:b, a:b]], axis=1)
                right = jnp.concatenate(
                    [
                        paired(qt_s[row, even * HEAD:even * HEAD + HEAD, a:b], True),
                        paired(qt_s[row, odd * HEAD:odd * HEAD + HEAD, a:b], False),
                    ],
                    axis=1,
                )
                dk_s[row, a:b, lanes] = (dot(left, right, 1, 1) * LN_2).astype(BF16)
                left = jnp.concatenate([probs[even, a:b, a:b], probs[odd, a:b, a:b]], axis=1)
                right = jnp.concatenate(
                    [paired(do_s[even % 4, :, a:b], True), paired(do_s[odd % 4, :, a:b], False)],
                    axis=1,
                )
                dv_s[row, a:b, lanes] = dot(left, right, 1, 1).astype(BF16)

        for step in range(pairs + 1):
            if step < pairs:
                score_grads(2 * step)
                score_grads(2 * step + 1)
            if step >= 1:
                grads(step - 1)

    def mean(value):
        return jnp.sum(value, axis=-1, keepdims=True) * (1.0 / width)

    def weave(main, side):
        for index, step in enumerate(main):
            step()
            for part in side[index * len(side) // len(main):(index + 1) * len(side) // len(main)]:
                part()

    chunks = hidden_units // CHUNK
    piece = 32

    def feed_forward(row):
        def blocks(half, body):
            start = half * tokens
            return [
                functools.partial(body, slice(at, at + piece))
                for at in range(start, start + tokens, piece)
            ]

        def span(half):
            return slice(half * tokens, (half + 1) * tokens)

        def attended(half):
            def step(at):
                acc_s[span(half), at] = dot(ctx_s[:, span(half)], wo_s[:, at], 0, 0)

            return [
                functools.partial(step, slice(at, at + 256)) for at in range(0, width, 256)
            ]

        def norm_one(at):
            resid = x_s[row, at, :].astype(F32) + acc_s[at, :]
            center = resid - mean(resid)
            scaled = lax.rsqrt(mean(center * center) + NORM_EPS)
            normed = center * scaled
            normed_s[at, :] = normed
            rstd_s[at, :] = scaled
            low16[at, :] = (normed * gain_one + shift_one).astype(BF16)

        def forward(half):
            here = span(half)

            def run(step):
                if step < chunks:
                    at = slice(step * CHUNK, (step + 1) * CHUNK)
                    score[step % 2, here, :] = dot(low16[here, :], wx_s[:, at], 1, 0)
                if 0 <= step - 1 < chunks:
                    at = slice((step - 1) * CHUNK, step * CHUNK)
                    inner = score[(step - 1) % 2, here, :]
                    upto = 0.5 + 0.5 * lax.erf(inner * math.sqrt(0.5))
                    bell = jnp.exp2(inner * inner * (-0.5 * LOG2_E)) * (
                        1.0 / math.sqrt(2.0 * math.pi)
                    )
                    act_s[(step - 1) % 2, here, :] = (inner * upto).astype(BF16)
                    slope_s[here, at] = (upto + inner * bell).astype(BF16)
                if 0 <= step - 2:
                    at = slice((step - 2) * CHUNK, (step - 1) * CHUNK)
                    part = dot(act_s[(step - 2) % 2, here, :], wr_s[at, :], 1, 0)
                    if step == 2:
                        acc_s[here, :] = part
                    else:
                        acc_s[here, :] += part

            return [functools.partial(run, step) for step in range(chunks + 2)]

        def norm_two(at):
            z = normed_s[at, :] * gain_one + shift_one + acc_s[at, :]
            center = z - mean(z)
            scaled = lax.rsqrt(mean(center * center) + NORM_EPS)
            normed = center * scaled
            lo_s[row, at, :] = (normed * gain_two + shift_two).astype(BF16)
            weighted = og_s[row, at, :].astype(F32) * gain_two
            grad = scaled * (weighted - mean(weighted) - normed * mean(weighted * normed))
            back_s[at, :] = grad
            low16[at, :] = grad.astype(BF16)

        def backward(half):
            here = span(half)

            def run(step):
                if step < chunks:
                    at = slice(step * CHUNK, (step + 1) * CHUNK)
                    part = dot(low16[here, :], wr_s[at, :], 1, 1)
                    act_s[step % 2, here, :] = (part * slope_s[here, at].astype(F32)).astype(BF16)
                if step >= 1:
                    at = slice((step - 1) * CHUNK, step * CHUNK)
                    part = dot(act_s[(step - 1) % 2, here, :], wx_s[:, at], 1, 1)
                    if step == 1:
                        acc_s[here, :] = part
                    else:
                        acc_s[here, :] += part

            return [functools.partial(run, step) for step in range(chunks + 1)]

        def norm_one_back(at):
            weighted = (back_s[at, :] + acc_s[at, :]) * gain_one
            normed = normed_s[at, :]
            grad = rstd_s[at, :] * (
                weighted - mean(weighted) - normed * mean(weighted * normed)
            )
            g_s[row, at, :] = grad.astype(BF16)

        def context_grad(half):
            def step(at):
                gctx_s[at, span(half)] = dot(wo_s[at, :], g_s[row, span(half), :], 1, 1)

            return [
                functools.partial(step, slice(at, at + 256)) for at in range(0, width, 256)
            ]

        def turn(half):
            def step(at):
                kt_s[at, span(half)] = k_s[row, span(half), at].T
                v_s[span(half), at] = vt_s[row, at, span(half)].T

            return [
                functools.partial(step, slice(at, at + 128)) for at in range(0, width, 128)
            ]

        weave(attended(0), [])
        weave(attended(1), blocks(0, norm_one))

        @pl.when(row == 0)
        def _():
            loads[9].wait()
            loads[10].wait()

        weave(forward(0), blocks(1, norm_one))

        @pl.when(row == 0)
        def _():
            loads[11].wait()
            loads[12].wait()

        weave(forward(1), blocks(0, norm_two))
        weave(backward(0), blocks(1, norm_two))
        weave(backward(1), blocks(0, norm_one_back) + turn(0) + turn(1))
        weave(context_grad(0), blocks(1, norm_one_back))
        weave(context_grad(1), [])

    def one_row(row, carry):
        own = rows * place + row
        position = (lax.broadcasted_iota(jnp.int32, (group, 128), 0) + place * tokens) % group
        lane = lax.broadcasted_iota(jnp.int32, (1, 128), 1)
        low = jnp.full((1, 128), group, jnp.int32)
        high = low
        across = lax.broadcasted_iota(jnp.int32, (slots, group), 1)
        across = (across + place * tokens) % group
        line = lax.broadcasted_iota(jnp.int32, (slots, 1), 0)
        first = jnp.full((slots, 1), group, jnp.int32)
        last = first
        start = jnp.int32(0)
        crossing = jnp.int32(0)
        for slot in range(slots):
            size = sizes[own, slot]
            live = lives[own, slot]
            low = jnp.where(lane == slot, start, low)
            high = jnp.where(lane == slot, start + live, high)
            first = jnp.where(line == slot, start, first)
            last = jnp.where(line == slot, start + size, last)
            over = (start < tokens) & (start + size > tokens)
            crossing = jnp.where(over, 1, crossing)
            start = start + size
        dead = jnp.where((position >= low) & (position < high), 0.0, 1.0)
        kmask[...] = jnp.where(lane < slots, dead, 0.0).astype(BF16)
        within = jnp.where((across >= first) & (across < last), MASK_FILL, 0.0)
        qmask[...] = jnp.concatenate(
            [within, jnp.zeros((128 - slots, group), F32)], axis=0
        ).astype(BF16)

        @pl.when(crossing == 1)
        def _():
            attend_forward(row, [(0, group)])

        @pl.when(crossing == 0)
        def _():
            attend_forward(row, [(0, tokens), (tokens, group)])

        @pl.when(row == 0)
        def _():
            loads[7].wait()
            loads[8].wait()

        feed_forward(row)

        @pl.when(crossing == 1)
        def _():
            attend_backward(row, [(0, group)])

        @pl.when(crossing == 0)
        def _():
            attend_backward(row, [(0, tokens), (tokens, group)])

        for copy in row_stores(row):
            copy.start()
        from_q = dot(low_s[row], dqt_s[row], 1, 1) * (
            ADAPTER_STRENGTH / slots_rank / math.sqrt(HEAD) / LN_2
        )
        from_v = dot(low_s[row], dv_s[row], 1, 0) * (ADAPTER_STRENGTH / slots_rank)
        rank_line = lax.broadcasted_iota(jnp.int32, (2 * slots_rank, 1), 0)
        part = jnp.where(rank_line < slots_rank, from_q, from_v)
        up_out[...] = jnp.where(row == 0, part, up_out[...] + part)
        return carry

    slots_rank = low_s.shape[1] // 2
    lax.fori_loop(0, rows, one_row, 0)
    for row in range(rows):
        for copy in row_stores(row):
            copy.wait()


def phases():
    found = [("seq", 1, 2)]
    stride, left = 1, lax.axis_size("dp")
    while left > 1:
        size = 4 if left % 4 == 0 else left if left < 4 else 2
        found.append(("dp", stride, size))
        stride, left = stride * size, left // size
    return found


def finish_kernel(
    up, lo, grad, dqt, dk, dv, wq, wk, wv,
    lo_out, ig_out, up_out,
    pair, got, lo_s, grad_s, dqt_s, dk_s, dv_s, wq_s, wk_s, wv_s, acc_s, res_s,
    load, store, send, recv, ar_send, ar_recv,
):
    rows, group, width = grad_s.shape
    tokens = group // 2
    place = lax.axis_index("seq")
    other = 1 - place
    plan = [
        (dqt, dqt_s), (wq, wq_s), (dk, dk_s), (wk, wk_s), (dv, dv_s), (wv, wv_s), (grad, grad_s),
        (lo, lo_s),
    ]
    loads = [
        pltpu.make_async_copy(source, target, load.at[index])
        for index, (source, target) in enumerate(plan)
    ]
    for copy in loads:
        copy.start()
    barrier = pltpu.get_barrier_semaphore()
    rounds = []
    greeted = 0
    for axis, stride, size in phases():
        me = lax.axis_index(axis)
        digit = (me // stride) % size
        others = []
        for step in range(1, size):
            theirs = (digit + step) % size
            others.append((theirs, {axis: me + (theirs - digit) * stride}))
        for _, device in others:
            pl.semaphore_signal(barrier, inc=1, device_id=device, device_id_type=MESH)
        greeted += len(others)
        rounds.append((size, digit, others))
    pl.semaphore_wait(barrier, greeted)
    mine = pl.ds(rows * place, rows)

    def copies(index):
        size, digit, others = rounds[index]
        buffer = pair if index == 0 else got.at[index - 1]
        sends = [
            pltpu.make_async_remote_copy(
                src_ref=buffer.at[digit], dst_ref=buffer.at[digit],
                send_sem=ar_send.at[index, step], recv_sem=ar_recv.at[index, digit],
                device_id=device, device_id_type=MESH,
            )
            for step, (_, device) in enumerate(others)
        ]
        arrivals = [
            pltpu.make_async_remote_copy(
                src_ref=buffer.at[theirs], dst_ref=buffer.at[theirs],
                send_sem=ar_send.at[index, step], recv_sem=ar_recv.at[index, theirs],
                device_id=device, device_id_type=MESH,
            )
            for step, (theirs, device) in enumerate(others)
        ]
        return sends, arrivals

    all_copies = [copies(index) for index in range(len(rounds))]

    def begin(index, value):
        digit = rounds[index][1]
        if index == 0:
            pair[digit] = value
        else:
            got[index - 1, digit] = value.astype(BF16)
        for copy in all_copies[index][0]:
            copy.start()

    def end(index):
        size = rounds[index][0]
        for copy in all_copies[index][1]:
            copy.wait_recv()
        buffer = pair if index == 0 else got.at[index - 1]
        value = buffer[0].astype(F32)
        for step in range(1, size):
            value = value + buffer[step].astype(F32)
        return value

    begin(0, up[...])
    done = [0]

    def advance():
        if done[0] < len(rounds):
            value = end(done[0])
            done[0] += 1
            if done[0] < len(rounds):
                begin(done[0], value)
            else:
                up_out[...] = value

    def from_q(half):
        span = slice(half * tokens, (half + 1) * tokens)
        left = jnp.concatenate([dqt_s[row, :, span] for row in range(rows)], axis=1)
        acc_s[...] = dot(left, wq_s[...], 0, 1)

    def from_k(half):
        left = dk_s[:, half * tokens:(half + 1) * tokens, :].reshape(rows * tokens, width)
        acc_s[...] += dot(left, wk_s[...], 1, 1)

    def from_v(half):
        span = slice(half * tokens, (half + 1) * tokens)
        left = dv_s[:, span, :].reshape(rows * tokens, width)
        value = acc_s[...] + dot(left, wv_s[...], 1, 1)
        value += grad_s[:, span, :].reshape(rows * tokens, width).astype(F32)
        res_s[half] = value.astype(BF16).reshape(rows, tokens, width)

    def sibling(source, target, index):
        return pltpu.make_async_remote_copy(
            src_ref=source, dst_ref=target, send_sem=send.at[index], recv_sem=recv.at[index],
            device_id={"seq": other}, device_id_type=MESH,
        )

    loads[0].wait()
    loads[1].wait()
    from_q(1)
    advance()
    loads[2].wait()
    loads[3].wait()
    from_k(1)
    for copy in loads[4:7]:
        copy.wait()
    from_v(1)
    ig_copy = sibling(res_s.at[1], ig_out.at[mine], 0)
    ig_copy.start()
    loads[7].wait()
    lo_copy = sibling(lo_s.at[:, pl.ds(tokens, tokens)], lo_out.at[mine], 1)
    lo_copy.start()
    keep_lo = pltpu.make_async_copy(lo_s.at[:, pl.ds(0, tokens)], lo_out.at[mine], store.at[0])
    keep_lo.start()
    from_q(0)
    advance()
    from_k(0)
    from_v(0)
    keep_ig = pltpu.make_async_copy(res_s.at[0], ig_out.at[mine], store.at[1])
    keep_ig.start()
    for _ in range(len(rounds)):
        advance()
    for sends, _ in all_copies:
        for copy in sends:
            copy.wait_send()
    keep_lo.wait()
    keep_ig.wait()
    lo_copy.wait()
    ig_copy.wait()


def widen_kernel(lo, ig, up, lo_out, ig_out, upq_out, upv_out, lo_s, ig_s, wide_s, load, store):
    micro = lo.shape[0]
    loads = [
        pltpu.make_async_copy(ig.at[index], ig_s.at[index], load.at[index])
        for index in range(micro)
    ]
    loads.append(pltpu.make_async_copy(lo, lo_s, load.at[micro]))
    for copy in loads:
        copy.start()
    stores = []
    for index in range(micro):
        loads[index].wait()
        wide_s[index] = ig_s[index].astype(F32)
        stores.append(pltpu.make_async_copy(wide_s.at[index], ig_out.at[index], store.at[index]))
        stores[-1].start()
    loads[micro].wait()
    stores.append(pltpu.make_async_copy(lo_s, lo_out, store.at[micro]))
    stores[-1].start()
    rank = upq_out.shape[0]
    upq_out[...] = up[:rank]
    upv_out[...] = up[rank:]
    for copy in stores:
        copy.wait()


def shards(
    hidden_in, slot_sizes, live_lengths, w_query, w_key, w_value, query_down_factor, down_value,
    query_up_factor, value_up_factor, w_output, attn_gain, attn_shift, w_expand, w_reduce,
    ffn_gain, ffn_shift, out_grad,
):
    micro, tokens, width = hidden_in.shape
    rows = micro // 2
    group = 2 * tokens
    hidden_units = w_expand.shape[1]
    rank = query_down_factor.shape[1]
    shape = jax.ShapeDtypeStruct
    dma = pltpu.SemaphoreType.DMA
    wide = (rows, width, group)
    tall = (rows, group, width)
    half_tall = (rows, tokens, width)
    half_wide = (rows, width, tokens)
    square = (width, width)
    limit = 62 * 2 ** 20
    down_q, down_v = query_down_factor.T, down_value.T
    x_got, og_got, qt, keys, vt, low, wq_eff, wv_eff = pl.pallas_call(
        exchange_kernel,
        out_shape=[
            shape(half_tall, BF16), shape(half_tall, BF16), shape(half_wide, BF16),
            shape(half_tall, BF16), shape(half_wide, BF16), shape((rows, 2 * rank, tokens), BF16),
            shape(square, BF16), shape(square, BF16),
        ],
        in_specs=[HBM_SPEC] * 5 + [VMEM_SPEC] * 4,
        out_specs=[HBM_SPEC] * 5 + [VMEM_SPEC] + [HBM_SPEC] * 2,
        scratch_shapes=[
            VMEM(half_tall, BF16), VMEM(square, BF16), VMEM(square, BF16), VMEM(square, BF16),
            VMEM(half_wide, BF16), VMEM(half_tall, BF16), VMEM(half_wide, BF16),
            dma((4,)), dma((5,)), dma((2,)), dma((2,)),
        ],
        compiler_params=pltpu.CompilerParams(
            collective_id=0, has_side_effects=True, vmem_limit_bytes=limit
        ),
        name="project",
    )(
        hidden_in, out_grad, w_query, w_key, w_value, down_q, down_v,
        query_up_factor, value_up_factor,
    )
    place = lax.axis_index("seq").astype(jnp.int32).reshape(1)
    lo, grad, dqt, dk, dv, up = pl.pallas_call(
        layer_kernel,
        out_shape=[
            shape(tall, BF16), shape(tall, BF16), shape(wide, BF16), shape(tall, BF16),
            shape(tall, BF16), shape((2 * rank, width), F32),
        ],
        in_specs=[SMEM_SPEC] * 3 + [VMEM_SPEC] * 7 + [HBM_SPEC] * 13,
        out_specs=[HBM_SPEC] * 5 + [VMEM_SPEC],
        scratch_shapes=[
            VMEM(tall, BF16), VMEM(tall, BF16), VMEM(wide, BF16), VMEM(tall, BF16),
            VMEM(wide, BF16), VMEM((width, group), BF16), VMEM((group, width), BF16),
            VMEM((rows, 2 * rank, group), BF16),
            VMEM(square, BF16), VMEM(square, BF16), VMEM(square, BF16),
            VMEM(square, BF16), VMEM((width, hidden_units), BF16),
            VMEM((hidden_units, width), BF16),
            VMEM((HEADS, group, group), BF16), VMEM((2, group, group), F32),
            VMEM((width, group), BF16), VMEM((16, group), F32), VMEM((width, group), F32),
            VMEM((group, width), F32), VMEM((group, width), F32), VMEM((group, width), F32),
            VMEM((group, width), BF16), VMEM((group, hidden_units), BF16),
            VMEM((2, group, CHUNK), BF16), VMEM((4, group, group), BF16),
            VMEM((4, HEAD, group), BF16), VMEM((group, 1), F32),
            VMEM((group, 128), BF16), VMEM((128, group), BF16),
            VMEM(tall, BF16), VMEM(tall, BF16), VMEM(wide, BF16), VMEM(tall, BF16),
            VMEM(tall, BF16),
            dma((13,)), dma((rows, 5)),
        ],
        compiler_params=pltpu.CompilerParams(vmem_limit_bytes=limit),
        name="layer",
    )(
        slot_sizes[0], live_lengths[0], place, attn_gain, attn_shift, ffn_gain, ffn_shift,
        low, down_q, down_v, hidden_in, out_grad, x_got, og_got,
        qt, keys, vt, wq_eff, w_key, wv_eff, w_output, w_expand, w_reduce,
    )
    count = len(phases())
    lo, ig, up = pl.pallas_call(
        finish_kernel,
        out_shape=[
            shape((micro, tokens, width), BF16), shape((micro, tokens, width), BF16),
            shape((2 * rank, width), F32),
        ],
        in_specs=[VMEM_SPEC] + [HBM_SPEC] * 8,
        out_specs=[HBM_SPEC] * 2 + [VMEM_SPEC],
        scratch_shapes=[
            VMEM((2, 2 * rank, width), F32), VMEM((count - 1, 4, 2 * rank, width), BF16),
            VMEM(tall, BF16),
            VMEM(tall, BF16), VMEM(wide, BF16), VMEM(tall, BF16), VMEM(tall, BF16),
            VMEM(square, BF16), VMEM(square, BF16), VMEM(square, BF16),
            VMEM((rows * tokens, width), F32), VMEM((2, rows, tokens, width), BF16),
            dma((8,)), dma((2,)), dma((2,)), dma((2,)), dma((count, 3)), dma((count, 4)),
        ],
        compiler_params=pltpu.CompilerParams(
            collective_id=1, has_side_effects=True, vmem_limit_bytes=limit
        ),
        name="finish",
    )(up, lo, grad, dqt, dk, dv, wq_eff, w_key, wv_eff)
    return pl.pallas_call(
        widen_kernel,
        out_shape=[
            shape(lo.shape, BF16), shape(ig.shape, F32),
            shape((rank, width), F32), shape((rank, width), F32),
        ],
        in_specs=[HBM_SPEC] * 2 + [VMEM_SPEC],
        out_specs=[HBM_SPEC] * 2 + [VMEM_SPEC] * 2,
        scratch_shapes=[
            VMEM(lo.shape, BF16), VMEM(ig.shape, BF16), VMEM(ig.shape, F32),
            dma((micro + 1,)), dma((micro + 1,)),
        ],
        compiler_params=pltpu.CompilerParams(vmem_limit_bytes=limit),
        name="widen",
    )(lo, ig, up)


def solution(mesh):
    tokens = P(None, ("dp", "seq"), None)
    table = P("dp", None, None)
    in_specs = (tokens, table, table) + (P(),) * 14 + (tokens,)
    out_specs = (tokens, tokens, P(), P())
    return jax.shard_map(shards, mesh=mesh, in_specs=in_specs, out_specs=out_specs, check_vma=False)
```

time: 106 us -> 80.2 us (0.76)
  Pallas kernels: 98.7 us -> 79.3 us
  other arithmetic: 3.45 us -> 0 us
  local copies, waits for them, and re-layouts: 2.37 us -> 0 us
    pallas_call x1, Pallas kernels: 30.7 us -> 16.4 us  [shards(): pl.pallas_call(finish_kernel, out_shape=[shape((micro, tokens, width), BF...]
    pallas_call x1, Pallas kernels: 57.5 us -> 50.9 us  [shards(): pl.pallas_call(layer_kernel, out_shape=[shape(tall, BF16), shape(tall, BF...]
    convert_element_type x1 -> x0, other arithmetic: 3.45 us -> none  [shards(): return (layer_out, input_grad.astype(F32), up_query_grad, up_value_grad)]
    unnamed x9 -> x0, local copies, waits for them, and re-layouts: 2.37 us -> none
    pallas_call x1 -> x2, Pallas kernels: 10.5 us -> 12 us  [the longest x1 7.27 us: shards(): pl.pallas_call(exchange_kernel, out_shape=[shape(half_tall, BF16), shape(...]
where the time goes in v1:
time: 80.2 us; the launch traced here: 80.1 us
  Pallas kernels  79.3 us (99%)
  between operations  0.84 us (1%)
    pallas_call x1, Pallas kernels, shards(): pl.pallas_call(layer_kernel, out_shape=[shape(tall, BF16), shape(tall, BF...  50.9 us
    pallas_call x1, Pallas kernels, shards(): pl.pallas_call(finish_kernel, out_shape=[shape((micro, tokens, width), BF...  16.4 us
    pallas_call x1, Pallas kernels, shards(): pl.pallas_call(exchange_kernel, out_shape=[shape(half_tall, BF16), shape(...  7.27 us
    pallas_call x1, Pallas kernels, shards(): pl.pallas_call(widen_kernel, out_shape=[shape(lo.shape, BF16), shape(ig.s...  4.73 us

profile of v1, /device:TPU:0, one launch (start us, length us, event | category | flops | bytes accessed | tf_op | source)
XLA Modules:
  0.0 80.1 jit_solution(17980745841298461249)
XLA Ops:
  0.6 7.3 %project.1 = (bf16[2,256,768]{2,1,0:T(8,128)(2,1)}, bf16[2,256,768]{2,1,0:T(8,128)(2,1)}, bf16[2,768,256]{2,1,0:T(8,128)(2,1)}, bf16[2,256,768]{2,1,0:T(8,128)(2...) custom-call(bf16[4,256,768]{2,1,0:T(8,128)(2,1)} %hidden.3, ...), custom_call_target="tpu_custom_call" | custom-call | tf_op jit(solution)/shard_map/project/pallas_call | solution.py:680
  7.9 50.9 %layer.1 = (bf16[2,512,768]{2,1,0:T(8,128)(2,1)}, bf16[2,512,768]{2,1,0:T(8,128)(2,1)}, bf16[2,768,512]{2,1,0:T(8,128)(2,1)}, bf16[2,512,768]{2,1,0:T(8,128)(2,1...) custom-call(s32[4,8]{1,0:T(4,128)} %bitcast.9, s32[4,8]{1,0:T(4,128)} %bitcast.10, s32[1]{0:T(128)} %bitcast.2.place_ref, ...), custom_call_target="tpu_custom_call" | custom-call | tf_op jit(solution)/shard_map/layer/pallas_call | solution.py:703
  58.8 16.4 %finish.1 = (bf16[4,256,768]{2,1,0:T(8,128)(2,1)}, bf16[4,256,768]{2,1,0:T(8,128)(2,1)}, f32[16,768]{1,0:T(8,128)}) custom-call(f32[16,768]{1,0:T(8,128)} %get-tuple-element.29.up, bf16[2,512,768]{2,1,0:T(8,128)(2,1)} %get-tuple-element.30.lo, bf16[2,512,768]{2,1,0:T(8,128)(2,1)} %get-tuple-element.31.grad, bf16[2,768,512]{2,1,0:T(8,128)(2,1)} %get-tuple-element.32.dqt, ...), custom_call_target="tpu_custom_call" | custom-call | tf_op jit(solution)/shard_map/finish/pallas_call | solution.py:737
  75.2 4.7 %widen.1 = (bf16[4,256,768]{2,1,0:T(8,128)(2,1)}, f32[4,256,768]{2,1,0:T(8,128)}, f32[8,768]{1,0:T(8,128)}, f32[8,768]{1,0:T(8,128)}) custom-call(bf16[4,256,768]{2,1,0:T(8,128)(2,1)} %get-tuple-element.35.lo, bf16[4,256,768]{2,1,0:T(8,128)(2,1)} %get-tuple-element.36.ig, f32[16,768]{1,0:T(8,128)} %get-tuple-element.37.up), custom_call_target="tpu_custom_call" | custom-call | tf_op jit(solution)/shard_map/widen/pallas_call | solution.py:758

commit v2 on v1

--- a/solution.py
+++ b/solution.py
@@ -32,9 +32,9 @@
 
 
 def exchange_kernel(
-    hidden, out_grad, wq, wk, wv, aq, av, bq, bv,
+    hidden, out_grad, wq, wk, wv, aq_in, av_in, bq_in, bv_in,
     x_out, og_out, qt_out, k_out, vt_out, low_out, wq_out, wv_out,
-    x_s, wq_s, wk_s, wv_s, qt_s, k_s, vt_s, load, store, send, recv,
+    x_s, wq_s, wk_s, wv_s, aq, av, bq, bv, qt_s, k_s, vt_s, low_s, load, store, send, recv,
 ):
     rows, tokens, width = x_s.shape
     place = lax.axis_index("seq")
@@ -42,7 +42,8 @@
     loads = [
         pltpu.make_async_copy(source, target, load.at[index])
         for index, (source, target) in enumerate([
-            (wq, wq_s), (hidden.at[pl.ds(rows * place, rows)], x_s), (wk, wk_s), (wv, wv_s),
+            (wk, wk_s), (hidden.at[pl.ds(rows * place, rows)], x_s), (aq_in, aq), (bq_in, bq),
+            (wq, wq_s), (av_in, av), (bv_in, bv), (wv, wv_s),
         ])
     ]
     for copy in loads:
@@ -69,32 +70,32 @@
         stores.append(copy)
 
     loads[0].wait()
+    loads[1].wait()
+    x = x_s[...].reshape(rows * tokens, width)
+    k_s[...] = dot(x, wk_s[...], 1, 0).astype(BF16).reshape(rows, tokens, width)
+    keep(k_s, k_out)
+    for copy in loads[2:5]:
+        copy.wait()
     wq_s[...] = (
         (wq_s[...].astype(F32) + strength * dot(aq[...], bq[...], 0, 0))
         * (LOG2_E / math.sqrt(HEAD))
     ).astype(BF16)
     keep(wq_s, wq_out)
-    loads[1].wait()
-    x = x_s[...].reshape(rows * tokens, width)
-    qt = dot(wq_s[...], x, 0, 1).astype(BF16)
-    for row in range(rows):
-        qt_s[row] = qt[:, row * tokens:(row + 1) * tokens]
-    keep(qt_s, qt_out)
-    loads[3].wait()
+    for copy in loads[5:8]:
+        copy.wait()
     wv_s[...] = (
         wv_s[...].astype(F32) + strength * dot(av[...], bv[...], 0, 0)
     ).astype(BF16)
     keep(wv_s, wv_out)
-    loads[2].wait()
-    k_s[...] = dot(x, wk_s[...], 1, 0).astype(BF16).reshape(rows, tokens, width)
-    keep(k_s, k_out)
-    vt = dot(wv_s[...], x, 0, 1).astype(BF16)
-    for row in range(rows):
-        vt_s[row] = vt[:, row * tokens:(row + 1) * tokens]
-    keep(vt_s, vt_out)
     low = jnp.concatenate([dot(aq[...], x, 1, 1), dot(av[...], x, 1, 1)], axis=0).astype(BF16)
     for row in range(rows):
-        low_out[row] = low[:, row * tokens:(row + 1) * tokens]
+        low_s[row] = low[:, row * tokens:(row + 1) * tokens]
+    keep(low_s, low_out)
+    for weight, target, out in ((wq_s, qt_s, qt_out), (wv_s, vt_s, vt_out)):
+        part = dot(weight[...], x, 0, 1).astype(BF16)
+        for row in range(rows):
+            target[row] = part[:, row * tokens:(row + 1) * tokens]
+        keep(target, out)
     for copy in stores:
         copy.wait()
     for copy in remote:
@@ -102,45 +103,54 @@
 
 
 def layer_kernel(
-    sizes, lives, place_ref, gain_one, shift_one, gain_two, shift_two, low_in, aq, av,
-    hidden, out_grad, x_in, og_in, qt_in, k_in, vt_in, wq_in, wk_in, wv_in, wo_in, wx_in, wr_in,
-    lo_out, g_out, dqt_out, dk_out, dv_out, up_out,
-    x_s, og_s, qt_s, k_s, vt_s, kt_s, v_s, low_s, wq_s, wk_s, wv_s, wo_s, wx_s, wr_s,
-    probs, score, ctx_s, inv_s, gctx_s, normed_s, back_s, acc_s, low16, slope_s, act_s, ds_s, do_s,
-    rstd_s, kmask, qmask, lo_s, g_s, dqt_s, dk_s, dv_s,
-    load, store,
+    sizes, lives, place_ref, *refs
 ):
+    (
+        gain_one, shift_one, gain_two, shift_two, low_in, aq_in, av_in,
+        hidden, out_grad, x_in, og_in, qt_in, k_in, vt_in, wq_in, wk_in, wv_in,
+        wo_in, wx_in, wr_in,
+        lo_out, g_out, dqt_out, dk_out, dv_out, up_out,
+        vec_s, aq, av, x_s, og_s, qt_s, k_s, vt_s, kt_s, v_s, low_s, wq_s, wk_s, wv_s,
+        wo_s, wx_s, wr_s, probs, score, ctx_s, inv_s, gctx_s, normed_s, back_s, acc_s, low16,
+        slope_s, act_s, ds_s, do_s, rstd_s, kmask, qmask, lo_s, g_s, dqt_s, dk_s, dv_s, up_s,
+        load, store,
+    ) = refs
     rows, group, width = x_s.shape
     tokens = group // 2
     hidden_units = wx_s.shape[1]
     place = place_ref[0]
     slots = sizes.shape[1]
     pairs = HEADS // 2
-    gain_one, shift_one, gain_two, shift_two = (
-        part[...].reshape(1, width) for part in (gain_one, shift_one, gain_two, shift_two)
-    )
     first = pl.ds(0, tokens)
     second = pl.ds(tokens, tokens)
     mine = pl.ds(rows * place, rows)
+    plan = [
+        (x_in, x_s.at[:, second]),
+        (wk_in, wk_s),
+        (wq_in, wq_s),
+        (wv_in, wv_s),
+        (qt_in, qt_s.at[:, :, first]),
+        (k_in, k_s.at[:, first]),
+        (vt_in, vt_s.at[:, :, first]),
+        (wo_in, wo_s),
+        (hidden.at[mine], x_s.at[:, first]),
+        (wx_in, wx_s),
+        (wr_in, wr_s),
+        (out_grad.at[mine], og_s.at[:, first]),
+        (og_in, og_s.at[:, second]),
+        (aq_in, aq),
+        (av_in, av),
+        (low_in, low_s.at[:, :, first]),
+    ] + [
+        (vector, vec_s.at[index])
+        for index, vector in enumerate((gain_one, shift_one, gain_two, shift_two))
+    ]
     loads = [
         pltpu.make_async_copy(source, target, load.at[index])
-        for index, (source, target) in enumerate([
-            (x_in, x_s.at[:, second]),
-            (wk_in, wk_s),
-            (wq_in, wq_s),
-            (wv_in, wv_s),
-            (qt_in, qt_s.at[:, :, first]),
-            (k_in, k_s.at[:, first]),
-            (vt_in, vt_s.at[:, :, first]),
-            (wo_in, wo_s),
-            (hidden.at[mine], x_s.at[:, first]),
-            (wx_in, wx_s),
-            (wr_in, wr_s),
-            (out_grad.at[mine], og_s.at[:, first]),
-            (og_in, og_s.at[:, second]),
-        ])
+        for index, (source, target) in enumerate(plan)
     ]
-    for copy in loads:
+    small = loads[13:]
+    for copy in loads[:2] + small + loads[2:13]:
         copy.start()
 
     def row_stores(row):
@@ -156,13 +166,46 @@
             for index, (source, target) in enumerate(plan)
         ]
 
+    def make_masks(row):
+        own = rows * place + row
+        position = (lax.broadcasted_iota(jnp.int32, (group, 128), 0) + place * tokens) % group
+        lane = lax.broadcasted_iota(jnp.int32, (1, 128), 1)
+        low_end = jnp.full((1, 128), group, jnp.int32)
+        high_end = low_end
+        across = lax.broadcasted_iota(jnp.int32, (slots, group), 1)
+        across = (across + place * tokens) % group
+        line = lax.broadcasted_iota(jnp.int32, (slots, 1), 0)
+        begin = jnp.full((slots, 1), group, jnp.int32)
+        last = begin
+        start = jnp.int32(0)
+        crossing = jnp.int32(0)
+        for slot in range(slots):
+            size = sizes[own, slot]
+            live = lives[own, slot]
+            low_end = jnp.where(lane == slot, start, low_end)
+            high_end = jnp.where(lane == slot, start + live, high_end)
+            begin = jnp.where(line == slot, start, begin)
+            last = jnp.where(line == slot, start + size, last)
+            over = (start < tokens) & (start + size > tokens)
+            crossing = jnp.where(over, 1, crossing)
+            start = start + size
+        dead = jnp.where((position >= low_end) & (position < high_end), 0.0, 1.0)
+        kmask[row] = jnp.where(lane < slots, dead, 0.0).astype(BF16)
+        within = jnp.where((across >= begin) & (across < last), MASK_FILL, 0.0)
+        qmask[row] = jnp.concatenate(
+            [within, jnp.zeros((128 - slots, group), F32)], axis=0
+        ).astype(BF16)
+        return crossing
+
+    crossings = [make_masks(row) for row in range(rows)]
     loads[0].wait()
     loads[1].wait()
     x = x_s[:, tokens:, :].reshape(rows * tokens, width)
     k_s[:, tokens:, :] = dot(x, wk_s[...], 1, 0).astype(BF16).reshape(rows, tokens, width)
+    for copy in small:
+        copy.wait()
     low = jnp.concatenate([dot(aq[...], x, 1, 1), dot(av[...], x, 1, 1)], axis=0).astype(BF16)
     for row in range(rows):
-        low_s[row, :, :tokens] = low_in[row]
         low_s[row, :, tokens:] = low[:, row * tokens:(row + 1) * tokens]
     for weight, target, copy in ((wq_s, qt_s, loads[2]), (wv_s, vt_s, loads[3])):
         copy.wait()
@@ -171,6 +214,10 @@
             target[row, :, tokens:] = part[:, row * tokens:(row + 1) * tokens]
     for copy in loads[4:7]:
         copy.wait()
+
+    gain_one, shift_one, gain_two, shift_two = (
+        vec_s[index].reshape(1, width) for index in range(4)
+    )
 
     def paired(top, bottom_zero):
         zero = jnp.zeros_like(top)
@@ -181,9 +228,9 @@
             pair, odd = divmod(head, 2)
             lanes = slice(pair * 128, pair * 128 + 128)
             query = qt_s[row, head * HEAD:(head + 1) * HEAD, :]
-            right = jnp.concatenate([paired(query, odd == 0), qmask[...]], axis=0)
+            right = jnp.concatenate([paired(query, odd == 0), qmask[row]], axis=0)
             for a, b in spans:
-                left = jnp.concatenate([k_s[row, a:b, lanes], kmask[a:b, :]], axis=1)
+                left = jnp.concatenate([k_s[row, a:b, lanes], kmask[row, a:b, :]], axis=1)
                 score[head % 2, a:b, a:b] = dot(left, right[:, a:b], 1, 0)
 
         def weights(head):
@@ -233,7 +280,6 @@
                 ds_s[slot, a:b, a:b] = (probs[head, a:b, a:b].astype(F32) * part).astype(BF16)
 
         def grads(pair):
-            lanes = slice(pair * 128, pair * 128 + 128)
             even, odd = 2 * pair, 2 * pair + 1
             for a, b in spans:
                 for head in (even, odd):
@@ -241,6 +287,7 @@
                     dqt_s[row, here, a:b] = (
                         dot(kt_s[here, a:b], ds_s[head % 4, a:b, a:b], 1, 0) * LN_2
                     ).astype(BF16)
+                lanes = slice(pair * 128, pair * 128 + 128)
                 left = jnp.concatenate([ds_s[even % 4, a:b, a:b], ds_s[odd % 4, a:b, a:b]], axis=1)
                 right = jnp.concatenate(
                     [
@@ -406,34 +453,7 @@
         weave(context_grad(1), [])
 
     def one_row(row, carry):
-        own = rows * place + row
-        position = (lax.broadcasted_iota(jnp.int32, (group, 128), 0) + place * tokens) % group
-        lane = lax.broadcasted_iota(jnp.int32, (1, 128), 1)
-        low = jnp.full((1, 128), group, jnp.int32)
-        high = low
-        across = lax.broadcasted_iota(jnp.int32, (slots, group), 1)
-        across = (across + place * tokens) % group
-        line = lax.broadcasted_iota(jnp.int32, (slots, 1), 0)
-        first = jnp.full((slots, 1), group, jnp.int32)
-        last = first
-        start = jnp.int32(0)
-        crossing = jnp.int32(0)
-        for slot in range(slots):
-            size = sizes[own, slot]
-            live = lives[own, slot]
-            low = jnp.where(lane == slot, start, low)
-            high = jnp.where(lane == slot, start + live, high)
-            first = jnp.where(line == slot, start, first)
-            last = jnp.where(line == slot, start + size, last)
-            over = (start < tokens) & (start + size > tokens)
-            crossing = jnp.where(over, 1, crossing)
-            start = start + size
-        dead = jnp.where((position >= low) & (position < high), 0.0, 1.0)
-        kmask[...] = jnp.where(lane < slots, dead, 0.0).astype(BF16)
-        within = jnp.where((across >= first) & (across < last), MASK_FILL, 0.0)
-        qmask[...] = jnp.concatenate(
-            [within, jnp.zeros((128 - slots, group), F32)], axis=0
-        ).astype(BF16)
+        crossing = jnp.where(row == 0, crossings[0], crossings[1])
 
         @pl.when(crossing == 1)
         def _():
@@ -449,6 +469,8 @@
             loads[8].wait()
 
         feed_forward(row)
+        for copy in row_stores(row)[:2]:
+            copy.start()
 
         @pl.when(crossing == 1)
         def _():
@@ -458,7 +480,7 @@
         def _():
             attend_backward(row, [(0, tokens), (tokens, group)])
 
-        for copy in row_stores(row):
+        for copy in row_stores(row)[2:]:
             copy.start()
         from_q = dot(low_s[row], dqt_s[row], 1, 1) * (
             ADAPTER_STRENGTH / slots_rank / math.sqrt(HEAD) / LN_2
@@ -466,14 +488,17 @@
         from_v = dot(low_s[row], dv_s[row], 1, 0) * (ADAPTER_STRENGTH / slots_rank)
         rank_line = lax.broadcasted_iota(jnp.int32, (2 * slots_rank, 1), 0)
         part = jnp.where(rank_line < slots_rank, from_q, from_v)
-        up_out[...] = jnp.where(row == 0, part, up_out[...] + part)
+        up_s[...] = jnp.where(row == 0, part, up_s[...] + part)
         return carry
 
     slots_rank = low_s.shape[1] // 2
     lax.fori_loop(0, rows, one_row, 0)
+    keep_up = pltpu.make_async_copy(up_s, up_out, load.at[0])
+    keep_up.start()
     for row in range(rows):
         for copy in row_stores(row):
             copy.wait()
+    keep_up.wait()
 
 
 def phases():
@@ -489,7 +514,7 @@
 def finish_kernel(
     up, lo, grad, dqt, dk, dv, wq, wk, wv,
     lo_out, ig_out, up_out,
-    pair, got, lo_s, grad_s, dqt_s, dk_s, dv_s, wq_s, wk_s, wv_s, acc_s, res_s,
+    up_s, pair, got, grad_s, dqt_s, dk_s, dv_s, wq_s, wk_s, wv_s, acc_s, res_s,
     load, store, send, recv, ar_send, ar_recv,
 ):
     rows, group, width = grad_s.shape
@@ -497,14 +522,14 @@
     place = lax.axis_index("seq")
     other = 1 - place
     plan = [
-        (dqt, dqt_s), (wq, wq_s), (dk, dk_s), (wk, wk_s), (dv, dv_s), (wv, wv_s), (grad, grad_s),
-        (lo, lo_s),
+        (dqt, dqt_s), (wq, wq_s), (dk, dk_s), (wk, wk_s), (dv, dv_s), (wv, wv_s),
+        (grad, grad_s), (up, up_s),
     ]
     loads = [
         pltpu.make_async_copy(source, target, load.at[index])
         for index, (source, target) in enumerate(plan)
     ]
-    for copy in loads:
+    for copy in loads[7:] + loads[:7]:
         copy.start()
     barrier = pltpu.get_barrier_semaphore()
     rounds = []
@@ -544,6 +569,13 @@
         ]
         return sends, arrivals
 
+    def sibling(source, target, index):
+        return pltpu.make_async_remote_copy(
+            src_ref=source, dst_ref=target, send_sem=send.at[index], recv_sem=recv.at[index],
+            device_id={"seq": other}, device_id_type=MESH,
+        )
+
+    keep_up = pltpu.make_async_copy(up_s, up_out, store.at[0])
     all_copies = [copies(index) for index in range(len(rounds))]
 
     def begin(index, value):
@@ -565,7 +597,10 @@
             value = value + buffer[step].astype(F32)
         return value
 
-    begin(0, up[...])
+    loads[7].wait()
+    begin(0, up_s[...])
+    lo_copy = sibling(lo.at[:, pl.ds(tokens, tokens)], lo_out, 1)
+    lo_copy.start()
     done = [0]
 
     def advance():
@@ -575,29 +610,26 @@
             if done[0] < len(rounds):
                 begin(done[0], value)
             else:
-                up_out[...] = value
+                up_s[...] = value
+                keep_up.start()
 
     def from_q(half):
         span = slice(half * tokens, (half + 1) * tokens)
         left = jnp.concatenate([dqt_s[row, :, span] for row in range(rows)], axis=1)
         acc_s[...] = dot(left, wq_s[...], 0, 1)
 
+    def part(source, weight, half):
+        left = source[:, half * tokens:(half + 1) * tokens, :].reshape(rows * tokens, width)
+        return dot(left, weight[...], 1, 1)
+
     def from_k(half):
-        left = dk_s[:, half * tokens:(half + 1) * tokens, :].reshape(rows * tokens, width)
-        acc_s[...] += dot(left, wk_s[...], 1, 1)
+        acc_s[...] += part(dk_s, wk_s, half)
 
     def from_v(half):
         span = slice(half * tokens, (half + 1) * tokens)
-        left = dv_s[:, span, :].reshape(rows * tokens, width)
-        value = acc_s[...] + dot(left, wv_s[...], 1, 1)
+        value = acc_s[...] + part(dv_s, wv_s, half)
         value += grad_s[:, span, :].reshape(rows * tokens, width).astype(F32)
         res_s[half] = value.astype(BF16).reshape(rows, tokens, width)
-
-    def sibling(source, target, index):
-        return pltpu.make_async_remote_copy(
-            src_ref=source, dst_ref=target, send_sem=send.at[index], recv_sem=recv.at[index],
-            device_id={"seq": other}, device_id_type=MESH,
-        )
 
     loads[0].wait()
     loads[1].wait()
@@ -611,11 +643,6 @@
     from_v(1)
     ig_copy = sibling(res_s.at[1], ig_out.at[mine], 0)
     ig_copy.start()
-    loads[7].wait()
-    lo_copy = sibling(lo_s.at[:, pl.ds(tokens, tokens)], lo_out.at[mine], 1)
-    lo_copy.start()
-    keep_lo = pltpu.make_async_copy(lo_s.at[:, pl.ds(0, tokens)], lo_out.at[mine], store.at[0])
-    keep_lo.start()
     from_q(0)
     advance()
     from_k(0)
@@ -627,34 +654,51 @@
     for sends, _ in all_copies:
         for copy in sends:
             copy.wait_send()
-    keep_lo.wait()
+    keep_up.wait()
     keep_ig.wait()
     lo_copy.wait()
     ig_copy.wait()
 
 
-def widen_kernel(lo, ig, up, lo_out, ig_out, upq_out, upv_out, lo_s, ig_s, wide_s, load, store):
-    micro = lo.shape[0]
+def widen_kernel(
+    place_ref, lo, lo_got, ig, up, lo_out, ig_out, upq_out, upv_out,
+    lo_s, ig_s, wide_s, up_s, load, store,
+):
+    micro, tokens, width = ig_s.shape
+    rows = micro // 2
+    place = place_ref[0]
+    own = pl.ds(rows * place, rows)
+    rest = pl.ds(rows * (1 - place), rows)
+    rank = upq_out.shape[0]
     loads = [
         pltpu.make_async_copy(ig.at[index], ig_s.at[index], load.at[index])
         for index in range(micro)
+    ] + [
+        pltpu.make_async_copy(up, up_s, load.at[micro]),
+        pltpu.make_async_copy(lo.at[:, pl.ds(0, tokens)], lo_s.at[0], load.at[micro + 1]),
+        pltpu.make_async_copy(lo_got, lo_s.at[1], load.at[micro + 2]),
     ]
-    loads.append(pltpu.make_async_copy(lo, lo_s, load.at[micro]))
     for copy in loads:
         copy.start()
-    stores = []
+    widened = [
+        pltpu.make_async_copy(wide_s.at[index], ig_out.at[index], store.at[index])
+        for index in range(micro)
+    ]
     for index in range(micro):
         loads[index].wait()
         wide_s[index] = ig_s[index].astype(F32)
-        stores.append(pltpu.make_async_copy(wide_s.at[index], ig_out.at[index], store.at[index]))
-        stores[-1].start()
-    loads[micro].wait()
-    stores.append(pltpu.make_async_copy(lo_s, lo_out, store.at[micro]))
-    stores[-1].start()
-    rank = upq_out.shape[0]
-    upq_out[...] = up[:rank]
-    upv_out[...] = up[rank:]
+        widened[index].start()
+    stores = [
+        pltpu.make_async_copy(up_s.at[pl.ds(0, rank)], upq_out, store.at[micro]),
+        pltpu.make_async_copy(up_s.at[pl.ds(rank, rank)], upv_out, store.at[micro + 1]),
+        pltpu.make_async_copy(lo_s.at[0], lo_out.at[own], store.at[micro + 2]),
+        pltpu.make_async_copy(lo_s.at[1], lo_out.at[rest], store.at[micro + 3]),
+    ]
+    for copy in loads[micro:]:
+        copy.wait()
     for copy in stores:
+        copy.start()
+    for copy in widened + stores:
         copy.wait()
 
 
@@ -684,12 +728,15 @@
             shape(half_tall, BF16), shape(half_wide, BF16), shape((rows, 2 * rank, tokens), BF16),
             shape(square, BF16), shape(square, BF16),
         ],
-        in_specs=[HBM_SPEC] * 5 + [VMEM_SPEC] * 4,
-        out_specs=[HBM_SPEC] * 5 + [VMEM_SPEC] + [HBM_SPEC] * 2,
+        in_specs=[HBM_SPEC] * 9,
+        out_specs=[HBM_SPEC] * 8,
         scratch_shapes=[
             VMEM(half_tall, BF16), VMEM(square, BF16), VMEM(square, BF16), VMEM(square, BF16),
+            VMEM((rank, width), BF16), VMEM((rank, width), BF16),
+            VMEM((rank, width), BF16), VMEM((rank, width), BF16),
             VMEM(half_wide, BF16), VMEM(half_tall, BF16), VMEM(half_wide, BF16),
-            dma((4,)), dma((5,)), dma((2,)), dma((2,)),
+            VMEM((rows, 2 * rank, tokens), BF16),
+            dma((8,)), dma((6,)), dma((2,)), dma((2,)),
         ],
         compiler_params=pltpu.CompilerParams(
             collective_id=0, has_side_effects=True, vmem_limit_bytes=limit
@@ -706,9 +753,10 @@
             shape(tall, BF16), shape(tall, BF16), shape(wide, BF16), shape(tall, BF16),
             shape(tall, BF16), shape((2 * rank, width), F32),
         ],
-        in_specs=[SMEM_SPEC] * 3 + [VMEM_SPEC] * 7 + [HBM_SPEC] * 13,
-        out_specs=[HBM_SPEC] * 5 + [VMEM_SPEC],
+        in_specs=[SMEM_SPEC] * 3 + [HBM_SPEC] * 20,
+        out_specs=[HBM_SPEC] * 6,
         scratch_shapes=[
+            VMEM((4, width), F32), VMEM((rank, width), BF16), VMEM((rank, width), BF16),
             VMEM(tall, BF16), VMEM(tall, BF16), VMEM(wide, BF16), VMEM(tall, BF16),
             VMEM(wide, BF16), VMEM((width, group), BF16), VMEM((group, width), BF16),
             VMEM((rows, 2 * rank, group), BF16),
@@ -721,10 +769,10 @@
             VMEM((group, width), BF16), VMEM((group, hidden_units), BF16),
             VMEM((2, group, CHUNK), BF16), VMEM((4, group, group), BF16),
             VMEM((4, HEAD, group), BF16), VMEM((group, 1), F32),
-            VMEM((group, 128), BF16), VMEM((128, group), BF16),
+            VMEM((rows, group, 128), BF16), VMEM((rows, 128, group), BF16),
             VMEM(tall, BF16), VMEM(tall, BF16), VMEM(wide, BF16), VMEM(tall, BF16),
-            VMEM(tall, BF16),
-            dma((13,)), dma((rows, 5)),
+            VMEM(tall, BF16), VMEM((2 * rank, width), F32),
+            dma((20,)), dma((rows, 5)),
         ],
         compiler_params=pltpu.CompilerParams(vmem_limit_bytes=limit),
         name="layer",
@@ -734,17 +782,17 @@
         qt, keys, vt, wq_eff, w_key, wv_eff, w_output, w_expand, w_reduce,
     )
     count = len(phases())
-    lo, ig, up = pl.pallas_call(
+    lo_got, ig, up = pl.pallas_call(
         finish_kernel,
         out_shape=[
-            shape((micro, tokens, width), BF16), shape((micro, tokens, width), BF16),
+            shape(half_tall, BF16), shape((micro, tokens, width), BF16),
             shape((2 * rank, width), F32),
         ],
-        in_specs=[VMEM_SPEC] + [HBM_SPEC] * 8,
-        out_specs=[HBM_SPEC] * 2 + [VMEM_SPEC],
+        in_specs=[HBM_SPEC] * 9,
+        out_specs=[HBM_SPEC] * 3,
         scratch_shapes=[
+            VMEM((2 * rank, width), F32),
             VMEM((2, 2 * rank, width), F32), VMEM((count - 1, 4, 2 * rank, width), BF16),
-            VMEM(tall, BF16),
             VMEM(tall, BF16), VMEM(wide, BF16), VMEM(tall, BF16), VMEM(tall, BF16),
             VMEM(square, BF16), VMEM(square, BF16), VMEM(square, BF16),
             VMEM((rows * tokens, width), F32), VMEM((2, rows, tokens, width), BF16),
@@ -758,18 +806,19 @@
     return pl.pallas_call(
         widen_kernel,
         out_shape=[
-            shape(lo.shape, BF16), shape(ig.shape, F32),
+            shape((micro, tokens, width), BF16), shape((micro, tokens, width), F32),
             shape((rank, width), F32), shape((rank, width), F32),
         ],
-        in_specs=[HBM_SPEC] * 2 + [VMEM_SPEC],
-        out_specs=[HBM_SPEC] * 2 + [VMEM_SPEC] * 2,
+        in_specs=[SMEM_SPEC] + [HBM_SPEC] * 4,
+        out_specs=[HBM_SPEC] * 4,
         scratch_shapes=[
-            VMEM(lo.shape, BF16), VMEM(ig.shape, BF16), VMEM(ig.shape, F32),
-            dma((micro + 1,)), dma((micro + 1,)),
+            VMEM((2,) + half_tall, BF16), VMEM((micro, tokens, width), BF16),
+            VMEM((micro, tokens, width), F32), VMEM((2 * rank, width), F32),
+            dma((micro + 3,)), dma((micro + 4,)),
         ],
         compiler_params=pltpu.CompilerParams(vmem_limit_bytes=limit),
         name="widen",
-    )(lo, ig, up)
+    )(place, lo, lo_got, ig, up)
 
 
 def solution(mesh):

time: 80.2 us -> 76.6 us (0.955)
  Pallas kernels: 79.3 us -> 75.3 us
    pallas_call x2, Pallas kernels: 21.1 us -> 18.5 us  [the longest x1 15.2 us: shards(): pl.pallas_call(finish_kernel, out_shape=[shape(half_tall, BF16), shape((m...]
    pallas_call x1, Pallas kernels: 7.27 us -> 6.4 us  [shards(): pl.pallas_call(exchange_kernel, out_shape=[shape(half_tall, BF16), shape(...]
where the time goes in v2:
time: 76.6 us; the launch traced here: 76.1 us
  Pallas kernels  75.3 us (98%)
  between operations  0.84 us (1%)
    pallas_call x1, Pallas kernels, shards(): pl.pallas_call(layer_kernel, out_shape=[shape(tall, BF16), shape(tall, BF...  50.3 us
    pallas_call x1, Pallas kernels, shards(): pl.pallas_call(finish_kernel, out_shape=[shape(half_tall, BF16), shape((m...  15.2 us
    pallas_call x1, Pallas kernels, shards(): pl.pallas_call(exchange_kernel, out_shape=[shape(half_tall, BF16), shape(...  6.4 us
    pallas_call x1, Pallas kernels, shards(): pl.pallas_call(widen_kernel, out_shape=[shape((micro, tokens, width), BF1...  3.37 us

profile of v2, /device:TPU:0, one launch (start us, length us, event | category | flops | bytes accessed | tf_op | source)
XLA Modules:
  0.0 76.1 jit_solution(5142987626126565166)
XLA Ops:
  0.6 6.4 %project.1 = (bf16[2,256,768]{2,1,0:T(8,128)(2,1)}, bf16[2,256,768]{2,1,0:T(8,128)(2,1)}, bf16[2,768,256]{2,1,0:T(8,128)(2,1)}, bf16[2,256,768]{2,1,0:T(8,128)(2...) custom-call(bf16[4,256,768]{2,1,0:T(8,128)(2,1)} %refs_7_.1, ...), custom_call_target="tpu_custom_call" | custom-call | tf_op jit(solution)/shard_map/project/pallas_call | solution.py:724
  7.0 50.3 %layer.1 = (bf16[2,512,768]{2,1,0:T(8,128)(2,1)}, bf16[2,512,768]{2,1,0:T(8,128)(2,1)}, bf16[2,768,512]{2,1,0:T(8,128)(2,1)}, bf16[2,512,768]{2,1,0:T(8,128)(2,1...) custom-call(s32[4,8]{1,0:T(4,128)} %bitcast.9, s32[4,8]{1,0:T(4,128)} %bitcast.10, s32[1]{0:T(128)} %bitcast.place_ref, ...), custom_call_target="tpu_custom_call" | custom-call | tf_op jit(solution)/shard_map/layer/pallas_call | solution.py:750
  57.4 15.2 %finish.1 = (bf16[2,256,768]{2,1,0:T(8,128)(2,1)}, bf16[4,256,768]{2,1,0:T(8,128)(2,1)}, f32[16,768]{1,0:T(8,128)}) custom-call(f32[16,768]{1,0:T(8,128)} %get-tuple-element.30.up, bf16[2,512,768]{2,1,0:T(8,128)(2,1)} %get-tuple-element.29.lo, bf16[2,512,768]{2,1,0:T(8,128)(2,1)} %get-tuple-element.31.grad, bf16[2,768,512]{2,1,0:T(8,128)(2,1)} %get-tuple-element.32.dqt, ...), custom_call_target="tpu_custom_call" | custom-call | tf_op jit(solution)/shard_map/finish/pallas_call | solution.py:785
  72.6 3.4 %widen.1 = (bf16[4,256,768]{2,1,0:T(8,128)(2,1)}, f32[4,256,768]{2,1,0:T(8,128)}, f32[8,768]{1,0:T(8,128)}, f32[8,768]{1,0:T(8,128)}) custom-call(s32[1]{0:T(128)} %bitcast.place_ref, bf16[2,512,768]{2,1,0:T(8,128)(2,1)} %get-tuple-element.29.lo, bf16[2,256,768]{2,1,0:T(8,128)(2,1)} %get-tuple-element.35.lo_got, bf16[4,256,768]{2,1,0:T(8,128)(2,1)} %get-tuple-element.36.ig, ...), custom_call_target="tpu_custom_call" | custom-call | tf_op jit(solution)/shard_map/widen/pallas_call | solution.py:806

commit v3 on v2

--- a/solution.py
+++ b/solution.py
@@ -34,7 +34,8 @@
 def exchange_kernel(
     hidden, out_grad, wq, wk, wv, aq_in, av_in, bq_in, bv_in,
     x_out, og_out, qt_out, k_out, vt_out, low_out, wq_out, wv_out,
-    x_s, wq_s, wk_s, wv_s, aq, av, bq, bv, qt_s, k_s, vt_s, low_s, load, store, send, recv,
+    x_s, wq_s, wk_s, wv_s, delta_s, aq, av, bq, bv, qt_s, k_s, vt_s, low_s,
+    load, store, send, recv,
 ):
     rows, tokens, width = x_s.shape
     place = lax.axis_index("seq")
@@ -42,8 +43,8 @@
     loads = [
         pltpu.make_async_copy(source, target, load.at[index])
         for index, (source, target) in enumerate([
-            (wk, wk_s), (hidden.at[pl.ds(rows * place, rows)], x_s), (aq_in, aq), (bq_in, bq),
-            (wq, wq_s), (av_in, av), (bv_in, bv), (wv, wv_s),
+            (aq_in, aq), (bq_in, bq), (av_in, av), (bv_in, bv),
+            (wk, wk_s), (hidden.at[pl.ds(rows * place, rows)], x_s), (wq, wq_s), (wv, wv_s),
         ])
     ]
     for copy in loads:
@@ -69,33 +70,41 @@
         copy.start()
         stores.append(copy)
 
-    loads[0].wait()
-    loads[1].wait()
+    for copy in loads[:4]:
+        copy.wait()
+    thirds = [slice(at, at + 256) for at in range(0, width, 256)]
+    for at in thirds:
+        delta_s[0, at, :] = dot(aq[:, at], bq[...], 0, 0) * strength
+        delta_s[1, at, :] = dot(av[:, at], bv[...], 0, 0) * strength
+    for copy in loads[4:]:
+        copy.wait()
     x = x_s[...].reshape(rows * tokens, width)
-    k_s[...] = dot(x, wk_s[...], 1, 0).astype(BF16).reshape(rows, tokens, width)
+
+    def fold(weight, index, scale, at):
+        weight[at, :] = ((weight[at, :].astype(F32) + delta_s[index, at, :]) * scale).astype(BF16)
+
+    def project(weight, target, at):
+        part = dot(weight[:, at], x, 0, 1).astype(BF16)
+        for row in range(rows):
+            target[row, at, :] = part[:, row * tokens:(row + 1) * tokens]
+
+    for at in thirds:
+        k_s[:, :, at] = dot(x, wk_s[:, at], 1, 0).astype(BF16).reshape(rows, tokens, 256)
+        fold(wq_s, 0, LOG2_E / math.sqrt(HEAD), at)
     keep(k_s, k_out)
-    for copy in loads[2:5]:
-        copy.wait()
-    wq_s[...] = (
-        (wq_s[...].astype(F32) + strength * dot(aq[...], bq[...], 0, 0))
-        * (LOG2_E / math.sqrt(HEAD))
-    ).astype(BF16)
     keep(wq_s, wq_out)
-    for copy in loads[5:8]:
-        copy.wait()
-    wv_s[...] = (
-        wv_s[...].astype(F32) + strength * dot(av[...], bv[...], 0, 0)
-    ).astype(BF16)
+    for at in thirds:
+        project(wq_s, qt_s, at)
+        fold(wv_s, 1, 1.0, at)
+    keep(qt_s, qt_out)
     keep(wv_s, wv_out)
     low = jnp.concatenate([dot(aq[...], x, 1, 1), dot(av[...], x, 1, 1)], axis=0).astype(BF16)
     for row in range(rows):
         low_s[row] = low[:, row * tokens:(row + 1) * tokens]
     keep(low_s, low_out)
-    for weight, target, out in ((wq_s, qt_s, qt_out), (wv_s, vt_s, vt_out)):
-        part = dot(weight[...], x, 0, 1).astype(BF16)
-        for row in range(rows):
-            target[row] = part[:, row * tokens:(row + 1) * tokens]
-        keep(target, out)
+    for at in thirds:
+        project(wv_s, vt_s, at)
+    keep(vt_s, vt_out)
     for copy in stores:
         copy.wait()
     for copy in remote:
@@ -157,10 +166,13 @@
         plan = [
             (lo_s.at[row], lo_out.at[row]),
             (g_s.at[row], g_out.at[row]),
-            (dqt_s.at[row], dqt_out.at[row]),
-            (dk_s.at[row], dk_out.at[row]),
-            (dv_s.at[row], dv_out.at[row]),
         ]
+        for at in (pl.ds(0, width // 2), pl.ds(width // 2, width // 2)):
+            plan += [
+                (dqt_s.at[row, at], dqt_out.at[row, at]),
+                (dk_s.at[row, :, at], dk_out.at[row, :, at]),
+                (dv_s.at[row, :, at], dv_out.at[row, :, at]),
+            ]
         return [
             pltpu.make_async_copy(source, target, store.at[row, index])
             for index, (source, target) in enumerate(plan)
@@ -310,6 +322,9 @@
                 score_grads(2 * step + 1)
             if step >= 1:
                 grads(step - 1)
+            if step == pairs // 2:
+                for copy in row_stores(row)[2:5]:
+                    copy.start()
 
     def mean(value):
         return jnp.sum(value, axis=-1, keepdims=True) * (1.0 / width)
@@ -434,17 +449,7 @@
         weave(attended(0), [])
         weave(attended(1), blocks(0, norm_one))
 
-        @pl.when(row == 0)
-        def _():
-            loads[9].wait()
-            loads[10].wait()
-
         weave(forward(0), blocks(1, norm_one))
-
-        @pl.when(row == 0)
-        def _():
-            loads[11].wait()
-            loads[12].wait()
 
         weave(forward(1), blocks(0, norm_two))
         weave(backward(0), blocks(1, norm_two))
@@ -465,8 +470,8 @@
 
         @pl.when(row == 0)
         def _():
-            loads[7].wait()
-            loads[8].wait()
+            for copy in loads[7:13]:
+                copy.wait()
 
         feed_forward(row)
         for copy in row_stores(row)[:2]:
@@ -480,7 +485,7 @@
         def _():
             attend_backward(row, [(0, tokens), (tokens, group)])
 
-        for copy in row_stores(row)[2:]:
+        for copy in row_stores(row)[5:]:
             copy.start()
         from_q = dot(low_s[row], dqt_s[row], 1, 1) * (
             ADAPTER_STRENGTH / slots_rank / math.sqrt(HEAD) / LN_2
@@ -643,8 +648,8 @@
     from_v(1)
     ig_copy = sibling(res_s.at[1], ig_out.at[mine], 0)
     ig_copy.start()
+    advance()
     from_q(0)
-    advance()
     from_k(0)
     from_v(0)
     keep_ig = pltpu.make_async_copy(res_s.at[0], ig_out.at[mine], store.at[1])
@@ -732,6 +737,7 @@
         out_specs=[HBM_SPEC] * 8,
         scratch_shapes=[
             VMEM(half_tall, BF16), VMEM(square, BF16), VMEM(square, BF16), VMEM(square, BF16),
+            VMEM((2, width, width), F32),
             VMEM((rank, width), BF16), VMEM((rank, width), BF16),
             VMEM((rank, width), BF16), VMEM((rank, width), BF16),
             VMEM(half_wide, BF16), VMEM(half_tall, BF16), VMEM(half_wide, BF16),
@@ -772,7 +778,7 @@
             VMEM((rows, group, 128), BF16), VMEM((rows, 128, group), BF16),
             VMEM(tall, BF16), VMEM(tall, BF16), VMEM(wide, BF16), VMEM(tall, BF16),
             VMEM(tall, BF16), VMEM((2 * rank, width), F32),
-            dma((20,)), dma((rows, 5)),
+            dma((20,)), dma((rows, 8)),
         ],
         compiler_params=pltpu.CompilerParams(vmem_limit_bytes=limit),
         name="layer",

time: 76.6 us -> 74.5 us (0.973)
  Pallas kernels: 75.3 us -> 73.1 us
    pallas_call x1, Pallas kernels: 50.3 us -> 42.8 us  [shards(): pl.pallas_call(layer_kernel, out_shape=[shape(tall, BF16), shape(tall, BF...]
    pallas_call x1, Pallas kernels: 15.2 us -> 20.9 us  [shards(): pl.pallas_call(finish_kernel, out_shape=[shape(half_tall, BF16), shape((m...]
where the time goes in v3:
time: 74.5 us; the launch traced here: 73.9 us
  Pallas kernels  73.1 us (98%)
  between operations  0.84 us (1%)
    pallas_call x1, Pallas kernels, shards(): pl.pallas_call(layer_kernel, out_shape=[shape(tall, BF16), shape(tall, BF...  42.8 us
    pallas_call x1, Pallas kernels, shards(): pl.pallas_call(finish_kernel, out_shape=[shape(half_tall, BF16), shape((m...  20.9 us
    pallas_call x1, Pallas kernels, shards(): pl.pallas_call(exchange_kernel, out_shape=[shape(half_tall, BF16), shape(...  5.99 us
    pallas_call x1, Pallas kernels, shards(): pl.pallas_call(widen_kernel, out_shape=[shape((micro, tokens, width), BF1...  3.37 us

profile of v3, /device:TPU:0, one launch (start us, length us, event | category | flops | bytes accessed | tf_op | source)
XLA Modules:
  0.0 73.9 jit_solution(9184383084334750159)
XLA Ops:
  0.6 6.0 %project.1 = (bf16[2,256,768]{2,1,0:T(8,128)(2,1)}, bf16[2,256,768]{2,1,0:T(8,128)(2,1)}, bf16[2,768,256]{2,1,0:T(8,128)(2,1)}, bf16[2,256,768]{2,1,0:T(8,128)(2...) custom-call(bf16[4,256,768]{2,1,0:T(8,128)(2,1)} %refs_7_.1, ...), custom_call_target="tpu_custom_call" | custom-call | tf_op jit(solution)/shard_map/project/pallas_call | solution.py:729
  6.6 42.8 %layer.1 = (bf16[2,512,768]{2,1,0:T(8,128)(2,1)}, bf16[2,512,768]{2,1,0:T(8,128)(2,1)}, bf16[2,768,512]{2,1,0:T(8,128)(2,1)}, bf16[2,512,768]{2,1,0:T(8,128)(2,1...) custom-call(s32[4,8]{1,0:T(4,128)} %bitcast.9, s32[4,8]{1,0:T(4,128)} %bitcast.10, s32[1]{0:T(128)} %bitcast.place_ref, ...), custom_call_target="tpu_custom_call" | custom-call | tf_op jit(solution)/shard_map/layer/pallas_call | solution.py:756
  49.5 20.9 %finish.1 = (bf16[2,256,768]{2,1,0:T(8,128)(2,1)}, bf16[4,256,768]{2,1,0:T(8,128)(2,1)}, f32[16,768]{1,0:T(8,128)}) custom-call(f32[16,768]{1,0:T(8,128)} %get-tuple-element.30.up, bf16[2,512,768]{2,1,0:T(8,128)(2,1)} %get-tuple-element.29.lo, bf16[2,512,768]{2,1,0:T(8,128)(2,1)} %get-tuple-element.31.grad, bf16[2,768,512]{2,1,0:T(8,128)(2,1)} %get-tuple-element.32.dqt, ...), custom_call_target="tpu_custom_call" | custom-call | tf_op jit(solution)/shard_map/finish/pallas_call | solution.py:791
  70.4 3.4 %widen.1 = (bf16[4,256,768]{2,1,0:T(8,128)(2,1)}, f32[4,256,768]{2,1,0:T(8,128)}, f32[8,768]{1,0:T(8,128)}, f32[8,768]{1,0:T(8,128)}) custom-call(s32[1]{0:T(128)} %bitcast.place_ref, bf16[2,512,768]{2,1,0:T(8,128)(2,1)} %get-tuple-element.29.lo, bf16[2,256,768]{2,1,0:T(8,128)(2,1)} %get-tuple-element.35.lo_got, bf16[4,256,768]{2,1,0:T(8,128)(2,1)} %get-tuple-element.36.ig, ...), custom_call_target="tpu_custom_call" | custom-call | tf_op jit(solution)/shard_map/widen/pallas_call | solution.py:812

commit v4 on v3

--- a/solution.py
+++ b/solution.py
@@ -32,9 +32,9 @@
 
 
 def exchange_kernel(
-    hidden, out_grad, wq, wk, wv, aq_in, av_in, bq_in, bv_in,
-    x_out, og_out, qt_out, k_out, vt_out, low_out, wq_out, wv_out,
-    x_s, wq_s, wk_s, wv_s, delta_s, aq, av, bq, bv, qt_s, k_s, vt_s, low_s,
+    hidden, out_grad, wq, wk, wv, aq, av, bq, bv,
+    x_out, og_out, qt_out, k_out, vt_out, low_out, wq_out, wv_out, down_out,
+    x_s, wq_s, wk_s, wv_s, delta_s, down_s, qt_s, k_s, vt_s, low_s,
     load, store, send, recv,
 ):
     rows, tokens, width = x_s.shape
@@ -43,11 +43,10 @@
     loads = [
         pltpu.make_async_copy(source, target, load.at[index])
         for index, (source, target) in enumerate([
-            (aq_in, aq), (bq_in, bq), (av_in, av), (bv_in, bv),
             (wk, wk_s), (hidden.at[pl.ds(rows * place, rows)], x_s), (wq, wq_s), (wv, wv_s),
         ])
     ]
-    for copy in loads:
+    for copy in loads[:2]:
         copy.start()
     barrier = pltpu.get_barrier_semaphore()
     pl.semaphore_signal(barrier, inc=1, device_id={"seq": other}, device_id_type=MESH)
@@ -70,13 +69,17 @@
         copy.start()
         stores.append(copy)
 
-    for copy in loads[:4]:
-        copy.wait()
+    for copy in loads[2:]:
+        copy.start()
     thirds = [slice(at, at + 256) for at in range(0, width, 256)]
     for at in thirds:
         delta_s[0, at, :] = dot(aq[:, at], bq[...], 0, 0) * strength
         delta_s[1, at, :] = dot(av[:, at], bv[...], 0, 0) * strength
-    for copy in loads[4:]:
+    down_s[...] = jnp.concatenate(
+        [aq[...].astype(F32), av[...].astype(F32)], axis=0
+    ).astype(BF16)
+    keep(down_s, down_out)
+    for copy in loads[:2]:
         copy.wait()
     x = x_s[...].reshape(rows * tokens, width)
 
@@ -90,6 +93,9 @@
 
     for at in thirds:
         k_s[:, :, at] = dot(x, wk_s[:, at], 1, 0).astype(BF16).reshape(rows, tokens, 256)
+    for copy in loads[2:]:
+        copy.wait()
+    for at in thirds:
         fold(wq_s, 0, LOG2_E / math.sqrt(HEAD), at)
     keep(k_s, k_out)
     keep(wq_s, wq_out)
@@ -98,7 +104,7 @@
         fold(wv_s, 1, 1.0, at)
     keep(qt_s, qt_out)
     keep(wv_s, wv_out)
-    low = jnp.concatenate([dot(aq[...], x, 1, 1), dot(av[...], x, 1, 1)], axis=0).astype(BF16)
+    low = dot(down_s[...], x, 1, 1).astype(BF16)
     for row in range(rows):
         low_s[row] = low[:, row * tokens:(row + 1) * tokens]
     keep(low_s, low_out)
@@ -115,11 +121,11 @@
     sizes, lives, place_ref, *refs
 ):
     (
-        gain_one, shift_one, gain_two, shift_two, low_in, aq_in, av_in,
+        gain_one, shift_one, gain_two, shift_two, low_in, down_in,
         hidden, out_grad, x_in, og_in, qt_in, k_in, vt_in, wq_in, wk_in, wv_in,
         wo_in, wx_in, wr_in,
-        lo_out, g_out, dqt_out, dk_out, dv_out, up_out,
-        vec_s, aq, av, x_s, og_s, qt_s, k_s, vt_s, kt_s, v_s, low_s, wq_s, wk_s, wv_s,
+        lo_out, lo_send, g_out, dqt_out, dk_out, dv_out, up_out,
+        vec_s, down_s, x_s, og_s, qt_s, k_s, vt_s, kt_s, v_s, low_s, wq_s, wk_s, wv_s,
         wo_s, wx_s, wr_s, probs, score, ctx_s, inv_s, gctx_s, normed_s, back_s, acc_s, low16,
         slope_s, act_s, ds_s, do_s, rstd_s, kmask, qmask, lo_s, g_s, dqt_s, dk_s, dv_s, up_s,
         load, store,
@@ -147,8 +153,7 @@
         (wr_in, wr_s),
         (out_grad.at[mine], og_s.at[:, first]),
         (og_in, og_s.at[:, second]),
-        (aq_in, aq),
-        (av_in, av),
+        (down_in, down_s),
         (low_in, low_s.at[:, :, first]),
     ] + [
         (vector, vec_s.at[index])
@@ -164,7 +169,8 @@
 
     def row_stores(row):
         plan = [
-            (lo_s.at[row], lo_out.at[row]),
+            (lo_s.at[row, first], lo_out.at[rows * place + row]),
+            (lo_s.at[row, second], lo_send.at[row]),
             (g_s.at[row], g_out.at[row]),
         ]
         for at in (pl.ds(0, width // 2), pl.ds(width // 2, width // 2)):
@@ -216,7 +222,7 @@
     k_s[:, tokens:, :] = dot(x, wk_s[...], 1, 0).astype(BF16).reshape(rows, tokens, width)
     for copy in small:
         copy.wait()
-    low = jnp.concatenate([dot(aq[...], x, 1, 1), dot(av[...], x, 1, 1)], axis=0).astype(BF16)
+    low = dot(down_s[...], x, 1, 1).astype(BF16)
     for row in range(rows):
         low_s[row, :, tokens:] = low[:, row * tokens:(row + 1) * tokens]
     for weight, target, copy in ((wq_s, qt_s, loads[2]), (wv_s, vt_s, loads[3])):
@@ -323,7 +329,7 @@
             if step >= 1:
                 grads(step - 1)
             if step == pairs // 2:
-                for copy in row_stores(row)[2:5]:
+                for copy in row_stores(row)[3:6]:
                     copy.start()
 
     def mean(value):
@@ -474,7 +480,7 @@
                 copy.wait()
 
         feed_forward(row)
-        for copy in row_stores(row)[:2]:
+        for copy in row_stores(row)[:3]:
             copy.start()
 
         @pl.when(crossing == 1)
@@ -485,7 +491,7 @@
         def _():
             attend_backward(row, [(0, tokens), (tokens, group)])
 
-        for copy in row_stores(row)[5:]:
+        for copy in row_stores(row)[6:]:
             copy.start()
         from_q = dot(low_s[row], dqt_s[row], 1, 1) * (
             ADAPTER_STRENGTH / slots_rank / math.sqrt(HEAD) / LN_2
@@ -604,7 +610,7 @@
 
     loads[7].wait()
     begin(0, up_s[...])
-    lo_copy = sibling(lo.at[:, pl.ds(tokens, tokens)], lo_out, 1)
+    lo_copy = sibling(lo, lo_out, 1)
     lo_copy.start()
     done = [0]
 
@@ -672,7 +678,6 @@
     micro, tokens, width = ig_s.shape
     rows = micro // 2
     place = place_ref[0]
-    own = pl.ds(rows * place, rows)
     rest = pl.ds(rows * (1 - place), rows)
     rank = upq_out.shape[0]
     loads = [
@@ -680,8 +685,7 @@
         for index in range(micro)
     ] + [
         pltpu.make_async_copy(up, up_s, load.at[micro]),
-        pltpu.make_async_copy(lo.at[:, pl.ds(0, tokens)], lo_s.at[0], load.at[micro + 1]),
-        pltpu.make_async_copy(lo_got, lo_s.at[1], load.at[micro + 2]),
+        pltpu.make_async_copy(lo_got, lo_s, load.at[micro + 1]),
     ]
     for copy in loads:
         copy.start()
@@ -696,8 +700,7 @@
     stores = [
         pltpu.make_async_copy(up_s.at[pl.ds(0, rank)], upq_out, store.at[micro]),
         pltpu.make_async_copy(up_s.at[pl.ds(rank, rank)], upv_out, store.at[micro + 1]),
-        pltpu.make_async_copy(lo_s.at[0], lo_out.at[own], store.at[micro + 2]),
-        pltpu.make_async_copy(lo_s.at[1], lo_out.at[rest], store.at[micro + 3]),
+        pltpu.make_async_copy(lo_s, lo_out.at[rest], store.at[micro + 2]),
     ]
     for copy in loads[micro:]:
         copy.wait()
@@ -726,23 +729,21 @@
     square = (width, width)
     limit = 62 * 2 ** 20
     down_q, down_v = query_down_factor.T, down_value.T
-    x_got, og_got, qt, keys, vt, low, wq_eff, wv_eff = pl.pallas_call(
+    x_got, og_got, qt, keys, vt, low, wq_eff, wv_eff, down = pl.pallas_call(
         exchange_kernel,
         out_shape=[
             shape(half_tall, BF16), shape(half_tall, BF16), shape(half_wide, BF16),
             shape(half_tall, BF16), shape(half_wide, BF16), shape((rows, 2 * rank, tokens), BF16),
-            shape(square, BF16), shape(square, BF16),
+            shape(square, BF16), shape(square, BF16), shape((2 * rank, width), BF16),
         ],
-        in_specs=[HBM_SPEC] * 9,
-        out_specs=[HBM_SPEC] * 8,
+        in_specs=[HBM_SPEC] * 5 + [VMEM_SPEC] * 4,
+        out_specs=[HBM_SPEC] * 9,
         scratch_shapes=[
             VMEM(half_tall, BF16), VMEM(square, BF16), VMEM(square, BF16), VMEM(square, BF16),
-            VMEM((2, width, width), F32),
-            VMEM((rank, width), BF16), VMEM((rank, width), BF16),
-            VMEM((rank, width), BF16), VMEM((rank, width), BF16),
+            VMEM((2, width, width), F32), VMEM((2 * rank, width), BF16),
             VMEM(half_wide, BF16), VMEM(half_tall, BF16), VMEM(half_wide, BF16),
             VMEM((rows, 2 * rank, tokens), BF16),
-            dma((8,)), dma((6,)), dma((2,)), dma((2,)),
+            dma((4,)), dma((7,)), dma((2,)), dma((2,)),
         ],
         compiler_params=pltpu.CompilerParams(
             collective_id=0, has_side_effects=True, vmem_limit_bytes=limit
@@ -753,16 +754,16 @@
         query_up_factor, value_up_factor,
     )
     place = lax.axis_index("seq").astype(jnp.int32).reshape(1)
-    lo, grad, dqt, dk, dv, up = pl.pallas_call(
+    lo, lo_send, grad, dqt, dk, dv, up = pl.pallas_call(
         layer_kernel,
         out_shape=[
-            shape(tall, BF16), shape(tall, BF16), shape(wide, BF16), shape(tall, BF16),
-            shape(tall, BF16), shape((2 * rank, width), F32),
+            shape((micro, tokens, width), BF16), shape(half_tall, BF16), shape(tall, BF16),
+            shape(wide, BF16), shape(tall, BF16), shape(tall, BF16), shape((2 * rank, width), F32),
         ],
-        in_specs=[SMEM_SPEC] * 3 + [HBM_SPEC] * 20,
-        out_specs=[HBM_SPEC] * 6,
+        in_specs=[SMEM_SPEC] * 3 + [HBM_SPEC] * 19,
+        out_specs=[HBM_SPEC] * 7,
         scratch_shapes=[
-            VMEM((4, width), F32), VMEM((rank, width), BF16), VMEM((rank, width), BF16),
+            VMEM((4, width), F32), VMEM((2 * rank, width), BF16),
             VMEM(tall, BF16), VMEM(tall, BF16), VMEM(wide, BF16), VMEM(tall, BF16),
             VMEM(wide, BF16), VMEM((width, group), BF16), VMEM((group, width), BF16),
             VMEM((rows, 2 * rank, group), BF16),
@@ -778,13 +779,13 @@
             VMEM((rows, group, 128), BF16), VMEM((rows, 128, group), BF16),
             VMEM(tall, BF16), VMEM(tall, BF16), VMEM(wide, BF16), VMEM(tall, BF16),
             VMEM(tall, BF16), VMEM((2 * rank, width), F32),
-            dma((20,)), dma((rows, 8)),
+            dma((19,)), dma((rows, 9)),
         ],
         compiler_params=pltpu.CompilerParams(vmem_limit_bytes=limit),
         name="layer",
     )(
         slot_sizes[0], live_lengths[0], place, attn_gain, attn_shift, ffn_gain, ffn_shift,
-        low, down_q, down_v, hidden_in, out_grad, x_got, og_got,
+        low, down, hidden_in, out_grad, x_got, og_got,
         qt, keys, vt, wq_eff, w_key, wv_eff, w_output, w_expand, w_reduce,
     )
     count = len(phases())
@@ -808,7 +809,7 @@
             collective_id=1, has_side_effects=True, vmem_limit_bytes=limit
         ),
         name="finish",
-    )(up, lo, grad, dqt, dk, dv, wq_eff, w_key, wv_eff)
+    )(up, lo_send, grad, dqt, dk, dv, wq_eff, w_key, wv_eff)
     return pl.pallas_call(
         widen_kernel,
         out_shape=[
@@ -818,10 +819,11 @@
         in_specs=[SMEM_SPEC] + [HBM_SPEC] * 4,
         out_specs=[HBM_SPEC] * 4,
         scratch_shapes=[
-            VMEM((2,) + half_tall, BF16), VMEM((micro, tokens, width), BF16),
+            VMEM(half_tall, BF16), VMEM((micro, tokens, width), BF16),
             VMEM((micro, tokens, width), F32), VMEM((2 * rank, width), F32),
-            dma((micro + 3,)), dma((micro + 4,)),
+            dma((micro + 2,)), dma((micro + 3,)),
         ],
+        input_output_aliases={1: 0},
         compiler_params=pltpu.CompilerParams(vmem_limit_bytes=limit),
         name="widen",
     )(place, lo, lo_got, ig, up)

time: 74.5 us -> 74.4 us (level)
  no operation moved by 1% of the time
where the time goes in v4:
time: 74.4 us; the launch traced here: 73.7 us
  Pallas kernels  72.8 us (98%)
  between operations  0.84 us (1%)
    pallas_call x1, Pallas kernels, shards(): pl.pallas_call(layer_kernel, out_shape=[shape((micro, tokens, width), BF1...  42.8 us
    pallas_call x1, Pallas kernels, shards(): pl.pallas_call(finish_kernel, out_shape=[shape(half_tall, BF16), shape((m...  20.8 us
    pallas_call x1, Pallas kernels, shards(): pl.pallas_call(exchange_kernel, out_shape=[shape(half_tall, BF16), shape(...  6.19 us
    pallas_call x1, Pallas kernels, shards(): pl.pallas_call(widen_kernel, out_shape=[shape((micro, tokens, width), BF1...  3.1 us

profile of v4, /device:TPU:0, one launch (start us, length us, event | category | flops | bytes accessed | tf_op | source)
XLA Modules:
  0.0 73.7 jit_solution(8605201510748715762)
XLA Ops:
  0.6 6.2 %project.1 = (bf16[2,256,768]{2,1,0:T(8,128)(2,1)}, bf16[2,256,768]{2,1,0:T(8,128)(2,1)}, bf16[2,768,256]{2,1,0:T(8,128)(2,1)}, bf16[2,256,768]{2,1,0:T(8,128)(2...) custom-call(bf16[4,256,768]{2,1,0:T(8,128)(2,1)} %refs_6_.1, ...), custom_call_target="tpu_custom_call" | custom-call | tf_op jit(solution)/shard_map/project/pallas_call | solution.py:732
  6.8 42.8 %layer.1 = (bf16[4,256,768]{2,1,0:T(8,128)(2,1)}, bf16[2,256,768]{2,1,0:T(8,128)(2,1)}, bf16[2,512,768]{2,1,0:T(8,128)(2,1)}, bf16[2,768,512]{2,1,0:T(8,128)(2,1...) custom-call(s32[4,8]{1,0:T(4,128)} %bitcast.7, s32[4,8]{1,0:T(4,128)} %bitcast.8, ...), custom_call_target="tpu_custom_call" | custom-call | tf_op jit(solution)/shard_map/layer/pallas_call | solution.py:757
  49.6 20.8 %finish.1 = (bf16[2,256,768]{2,1,0:T(8,128)(2,1)}, bf16[4,256,768]{2,1,0:T(8,128)(2,1)}, f32[16,768]{1,0:T(8,128)}) custom-call(f32[16,768]{1,0:T(8,128)} %get-tuple-element.33.up, bf16[2,256,768]{2,1,0:T(8,128)(2,1)} %get-tuple-element.34.lo, bf16[2,512,768]{2,1,0:T(8,128)(2,1)} %get-tuple-element.35.grad, bf16[2,768,512]{2,1,0:T(8,128)(2,1)} %get-tuple-element.36.dqt, ...), custom_call_target="tpu_custom_call" | custom-call | tf_op jit(solution)/shard_map/finish/pallas_call | solution.py:792
  70.4 3.1 %widen.1 = (bf16[4,256,768]{2,1,0:T(8,128)(2,1)}, f32[4,256,768]{2,1,0:T(8,128)}, f32[8,768]{1,0:T(8,128)}, f32[8,768]{1,0:T(8,128)}) custom-call(s32[1]{0:T(128)} %bitcast.place_ref, bf16[4,256,768]{2,1,0:T(8,128)(2,1)} %get-tuple-element.32.lo, bf16[2,256,768]{2,1,0:T(8,128)(2,1)} %get-tuple-element.39.lo_got, ...), custom_call_target="tpu_custom_call", output_to_operand_aliasing={{0}: (1, {})} | custom-call | tf_op jit(solution)/shard_map/widen/pallas_call | solution.py:813

commit v5 on v4

--- a/solution.py
+++ b/solution.py
@@ -559,13 +559,16 @@
     pl.semaphore_wait(barrier, greeted)
     mine = pl.ds(rows * place, rows)
 
-    def copies(index):
-        size, digit, others = rounds[index]
-        buffer = pair if index == 0 else got.at[index - 1]
+    def buffer_of(index, half):
+        return pair if index == 0 else got.at[index - 1, half]
+
+    def copies(index, half):
+        _, digit, others = rounds[index]
+        buffer = buffer_of(index, half)
         sends = [
             pltpu.make_async_remote_copy(
                 src_ref=buffer.at[digit], dst_ref=buffer.at[digit],
-                send_sem=ar_send.at[index, step], recv_sem=ar_recv.at[index, digit],
+                send_sem=ar_send.at[index, half, step], recv_sem=ar_recv.at[index, half, digit],
                 device_id=device, device_id_type=MESH,
             )
             for step, (_, device) in enumerate(others)
@@ -573,7 +576,7 @@
         arrivals = [
             pltpu.make_async_remote_copy(
                 src_ref=buffer.at[theirs], dst_ref=buffer.at[theirs],
-                send_sem=ar_send.at[index, step], recv_sem=ar_recv.at[index, theirs],
+                send_sem=ar_send.at[index, half, step], recv_sem=ar_recv.at[index, half, theirs],
                 device_id=device, device_id_type=MESH,
             )
             for step, (theirs, device) in enumerate(others)
@@ -587,41 +590,46 @@
         )
 
     keep_up = pltpu.make_async_copy(up_s, up_out, store.at[0])
-    all_copies = [copies(index) for index in range(len(rounds))]
-
-    def begin(index, value):
-        digit = rounds[index][1]
-        if index == 0:
-            pair[digit] = value
-        else:
-            got[index - 1, digit] = value.astype(BF16)
-        for copy in all_copies[index][0]:
-            copy.start()
-
-    def end(index):
-        size = rounds[index][0]
-        for copy in all_copies[index][1]:
-            copy.wait_recv()
-        buffer = pair if index == 0 else got.at[index - 1]
-        value = buffer[0].astype(F32)
-        for step in range(1, size):
-            value = value + buffer[step].astype(F32)
-        return value
+    last = len(rounds) - 1
+    turns = [[(0, 0)]] + [[(1 + turn, 0), (last - turn, 1)] for turn in range(last)]
+    all_copies = [[copies(index, half) for index, half in turn] for turn in turns]
+
+    def begin(turn, values):
+        for (index, half), value, (sends, _) in zip(turns[turn], values, all_copies[turn]):
+            buffer_of(index, half)[rounds[index][1]] = value.astype(
+                F32 if index == 0 else BF16
+            )
+            for copy in sends:
+                copy.start()
+
+    def end(turn):
+        values = []
+        for (index, half), (_, arrivals) in zip(turns[turn], all_copies[turn]):
+            for copy in arrivals:
+                copy.wait_recv()
+            buffer = buffer_of(index, half)
+            value = buffer[0].astype(F32)
+            for step in range(1, rounds[index][0]):
+                value = value + buffer[step].astype(F32)
+            values.append(value)
+        return values
 
     loads[7].wait()
-    begin(0, up_s[...])
+    begin(0, [up_s[...]])
     lo_copy = sibling(lo, lo_out, 1)
     lo_copy.start()
     done = [0]
 
     def advance():
-        if done[0] < len(rounds):
-            value = end(done[0])
+        if done[0] < len(turns):
+            values = end(done[0])
             done[0] += 1
-            if done[0] < len(rounds):
-                begin(done[0], value)
+            if done[0] == 1:
+                values = [values[0][:, :width // 2], values[0][:, width // 2:]]
+            if done[0] < len(turns):
+                begin(done[0], values)
             else:
-                up_s[...] = value
+                up_s[...] = jnp.concatenate(values, axis=1)
                 keep_up.start()
 
     def from_q(half):
@@ -662,9 +670,10 @@
     keep_ig.start()
     for _ in range(len(rounds)):
         advance()
-    for sends, _ in all_copies:
-        for copy in sends:
-            copy.wait_send()
+    for turn in all_copies:
+        for sends, _ in turn:
+            for copy in sends:
+                copy.wait_send()
     keep_up.wait()
     keep_ig.wait()
     lo_copy.wait()
@@ -799,11 +808,11 @@
         out_specs=[HBM_SPEC] * 3,
         scratch_shapes=[
             VMEM((2 * rank, width), F32),
-            VMEM((2, 2 * rank, width), F32), VMEM((count - 1, 4, 2 * rank, width), BF16),
+            VMEM((2, 2 * rank, width), F32), VMEM((count - 1, 2, 4, 2 * rank, width // 2), BF16),
             VMEM(tall, BF16), VMEM(wide, BF16), VMEM(tall, BF16), VMEM(tall, BF16),
             VMEM(square, BF16), VMEM(square, BF16), VMEM(square, BF16),
             VMEM((rows * tokens, width), F32), VMEM((2, rows, tokens, width), BF16),
-            dma((8,)), dma((2,)), dma((2,)), dma((2,)), dma((count, 3)), dma((count, 4)),
+            dma((8,)), dma((2,)), dma((2,)), dma((2,)), dma((count, 2, 3)), dma((count, 2, 4)),
         ],
         compiler_params=pltpu.CompilerParams(
             collective_id=1, has_side_effects=True, vmem_limit_bytes=limit

time: 74.4 us -> 74.8 us (level)
  Pallas kernels: 72.8 us -> 73.6 us
    pallas_call x1, Pallas kernels: 42.8 us -> 48.5 us  [shards(): pl.pallas_call(layer_kernel, out_shape=[shape((micro, tokens, width), BF1...]
    pallas_call x1, Pallas kernels: 20.8 us -> 15.8 us  [shards(): pl.pallas_call(finish_kernel, out_shape=[shape(half_tall, BF16), shape((m...]
where the time goes in v5:
time: 74.8 us; the launch traced here: 74.4 us
  Pallas kernels  73.6 us (98%)
  between operations  0.84 us (1%)
    pallas_call x1, Pallas kernels, shards(): pl.pallas_call(layer_kernel, out_shape=[shape((micro, tokens, width), BF1...  48.5 us
    pallas_call x1, Pallas kernels, shards(): pl.pallas_call(finish_kernel, out_shape=[shape(half_tall, BF16), shape((m...  15.8 us
    pallas_call x1, Pallas kernels, shards(): pl.pallas_call(exchange_kernel, out_shape=[shape(half_tall, BF16), shape(...  6.19 us
    pallas_call x1, Pallas kernels, shards(): pl.pallas_call(widen_kernel, out_shape=[shape((micro, tokens, width), BF1...  3.1 us

profile of v5, /device:TPU:0, one launch (start us, length us, event | category | flops | bytes accessed | tf_op | source)
XLA Modules:
  0.0 74.4 jit_solution(2472475131378402481)
XLA Ops:
  0.6 6.2 %project.1 = (bf16[2,256,768]{2,1,0:T(8,128)(2,1)}, bf16[2,256,768]{2,1,0:T(8,128)(2,1)}, bf16[2,768,256]{2,1,0:T(8,128)(2,1)}, bf16[2,256,768]{2,1,0:T(8,128)(2...) custom-call(bf16[4,256,768]{2,1,0:T(8,128)(2,1)} %refs_6_.1, ...), custom_call_target="tpu_custom_call" | custom-call | tf_op jit(solution)/shard_map/project/pallas_call | solution.py:741
  6.8 48.5 %layer.1 = (bf16[4,256,768]{2,1,0:T(8,128)(2,1)}, bf16[2,256,768]{2,1,0:T(8,128)(2,1)}, bf16[2,512,768]{2,1,0:T(8,128)(2,1)}, bf16[2,768,512]{2,1,0:T(8,128)(2,1...) custom-call(s32[4,8]{1,0:T(4,128)} %bitcast.7, s32[4,8]{1,0:T(4,128)} %bitcast.8, ...), custom_call_target="tpu_custom_call" | custom-call | tf_op jit(solution)/shard_map/layer/pallas_call | solution.py:766
  55.3 15.8 %finish.1 = (bf16[2,256,768]{2,1,0:T(8,128)(2,1)}, bf16[4,256,768]{2,1,0:T(8,128)(2,1)}, f32[16,768]{1,0:T(8,128)}) custom-call(f32[16,768]{1,0:T(8,128)} %get-tuple-element.33.up, bf16[2,256,768]{2,1,0:T(8,128)(2,1)} %get-tuple-element.34.lo, bf16[2,512,768]{2,1,0:T(8,128)(2,1)} %get-tuple-element.35.grad, bf16[2,768,512]{2,1,0:T(8,128)(2,1)} %get-tuple-element.36.dqt, ...), custom_call_target="tpu_custom_call" | custom-call | tf_op jit(solution)/shard_map/finish/pallas_call | solution.py:801
  71.2 3.1 %widen.1 = (bf16[4,256,768]{2,1,0:T(8,128)(2,1)}, f32[4,256,768]{2,1,0:T(8,128)}, f32[8,768]{1,0:T(8,128)}, f32[8,768]{1,0:T(8,128)}) custom-call(s32[1]{0:T(128)} %bitcast.place_ref, bf16[4,256,768]{2,1,0:T(8,128)(2,1)} %get-tuple-element.32.lo, bf16[2,256,768]{2,1,0:T(8,128)(2,1)} %get-tuple-element.39.lo_got, ...), custom_call_target="tpu_custom_call", output_to_operand_aliasing={{0}: (1, {})} | custom-call | tf_op jit(solution)/shard_map/widen/pallas_call | solution.py:822
